TPU v7x, 32 devices: a whole 2x2x4 slice. The times are simulated.
32 devices in a mesh: groups: 2 (over x), req: 8 (over z, y), head: 2 (over core).
Axes of the slice: x: 2, y: 2, z: 4, core: 2. Of those that a mesh axis runs over, the one named last changes fastest.
Arguments:
- queries: bfloat16 [2048, 32, 128], P(('groups', 'req'), 'head'), parts along dimension 0, may hold values from -100 to 100
- new_keys: bfloat16 [2048, 2, 128], P(('groups', 'req'), 'head'), parts along dimension 0, may hold values from -4.5 to 4.5
- new_values: bfloat16 [2048, 2, 128], P(('groups', 'req'), 'head'), parts along dimension 0, may hold values from -6 to 6
- cluster_kv: bfloat16 [1024, 2, 2, 128, 128], P(('groups', 'req'), 'head'), parts along dimension 0, may hold values from -6 to 6
- cluster_len: int32 [32], P('groups'), parts along dimension 0, may hold values from 1 to 4096, 40960 in all
- piece_slot: int32 [32, 32], P('groups'), parts along dimension 0, may hold values from 0 to 511, as said below
- cluster_ids: int32 [16, 2, 2], P('groups', 'head'), parts along dimension 0, may hold values from 0 to 15, all different within a row
- w_out: bfloat16 [4096, 4096], P('head', 'req'), may hold values from -0.09375 to 0.09375
Outputs:
- projected: bfloat16 [2048, 4096], P(('groups', 'req', 'head')), parts along dimension 0
There are 2 independent parts, one for each index of `groups`. A program takes and returns all parts, laid end to end along the dimension named above; an argument that names none is the same for every part. Nothing has to cross between parts.
Inputs may be any that keep to these rules, and one draw needn't show every extreme that they name: `cluster_ids`: for each request and KV head, 2 distinct cluster numbers. A permutation of the slots: piece p of cluster c lies in slot piece_slot[c, p], stored on index slot // 64 of req, and every cluster has exactly 4 of its pieces on every index of req.
All inputs are finite; a program needn't handle non-finite values.
Results may differ from a plain program's by a relative error of at most 0.0052.
Values may be sent and summed in bfloat16 or wider, within the bound.
No kernel may reach another device: no remote copies, remote signals or barrier semaphores. Data moves between devices by JAX's collectives and lax.ppermute only.
A program may use at most 128 MiB of HBM per device.

v0:
```python
import jax
import jax.numpy as jnp
from jax import lax
from jax.sharding import PartitionSpec as P


def local(queries, new_keys, new_values, cluster_kv, cluster_len, piece_slot, cluster_ids, w_out):
    my_index = lax.axis_index("req")
    peers = lax.axis_size("req")
    tok_rows = queries.shape[0]
    head_count = queries.shape[1]
    head_size = queries.shape[2]
    held_slots = cluster_kv.shape[0]
    piece_keys = cluster_kv.shape[3]
    pieces = piece_slot.shape[1]
    per_peer = pieces // peers
    scale_factor = head_size ** (-0.5)
    plan_rows = cluster_ids[:, 0, :]
    owner_of = piece_slot // held_slots
    local_of = piece_slot % held_slots
    piece_pos = jnp.arange(pieces, dtype=jnp.int32)
    earlier = piece_pos[:, None] > piece_pos[None, :]
    rank_of = jnp.sum(
        ((owner_of[:, :, None] == owner_of[:, None, :]) & earlier[None]).astype(jnp.int32), axis=2
    )
    rank_choice = jnp.arange(per_peer, dtype=jnp.int32)
    held_here = (
        (owner_of == my_index)[:, :, None] & (rank_of[:, :, None] == rank_choice[None, None, :])
    ).astype(jnp.int32)
    send_table = jnp.sum(held_here * local_of[:, :, None], axis=1)
    send_slots = send_table[plan_rows]
    outgoing = cluster_kv[:, 0][send_slots]
    incoming = lax.all_to_all(outgoing, "req", split_axis=0, concat_axis=0, tiled=True)
    my_plan = lax.dynamic_index_in_dim(plan_rows, my_index, 0, keepdims=False)
    my_owner = owner_of[my_plan]
    my_rank = rank_of[my_plan]
    peer_pos = jnp.arange(peers, dtype=jnp.int32)
    matches = (my_owner[None, :, None, :] == peer_pos[:, None, None, None]) & (
        my_rank[None, :, None, :] == rank_choice[None, None, :, None]
    )
    piece_at = jnp.sum(matches.astype(jnp.int32) * piece_pos[None, None, None, :], axis=3)
    fill_limit = cluster_len[my_plan]
    key_pos = jnp.arange(piece_keys, dtype=jnp.int32)
    valid_keys = (
        piece_at[:, :, :, None] * piece_keys + key_pos[None, None, None, :]
        < fill_limit[None, :, None, None]
    ).reshape(-1)
    cached_keys = incoming[:, :, :, 0].reshape(-1, head_size)
    cached_values = incoming[:, :, :, 1].reshape(-1, head_size)
    position = jnp.arange(tok_rows, dtype=jnp.int32)
    causal = position[:, None] >= position[None, :]
    own_keys = new_keys[:, 0]
    own_values = new_values[:, 0]
    head_block = min(head_count, max(1, 512 // tok_rows))
    block_count = head_count // head_block
    causal_rows = jnp.tile(causal, (head_block, 1))

    def one_block(block_index):
        query_rows = lax.dynamic_slice_in_dim(queries, block_index * head_block, head_block, 1)
        query_rows = jnp.transpose(query_rows, (1, 0, 2)).reshape(head_block * tok_rows, head_size)
        cached_scores = (
            jnp.dot(query_rows, cached_keys.T, preferred_element_type=jnp.float32) * scale_factor
        )
        cached_scores = jnp.where(valid_keys[None, :], cached_scores, -jnp.inf)
        own_scores = (
            jnp.dot(query_rows, own_keys.T, preferred_element_type=jnp.float32) * scale_factor
        )
        own_scores = jnp.where(causal_rows, own_scores, -jnp.inf)
        row_top = jnp.maximum(jnp.max(cached_scores, axis=1), jnp.max(own_scores, axis=1))
        cached_weights = jnp.exp(cached_scores - row_top[:, None])
        own_weights = jnp.exp(own_scores - row_top[:, None])
        row_total = jnp.sum(cached_weights, axis=1) + jnp.sum(own_weights, axis=1)
        mixed_sum = jnp.dot(
            cached_weights.astype(jnp.bfloat16), cached_values, preferred_element_type=jnp.float32
        )
        mixed_sum = mixed_sum + jnp.dot(
            own_weights.astype(jnp.bfloat16), own_values, preferred_element_type=jnp.float32
        )
        result = (mixed_sum / row_total[:, None]).astype(jnp.bfloat16)
        return result.reshape(head_block, tok_rows, head_size)

    attended = lax.map(one_block, jnp.arange(block_count, dtype=jnp.int32)).reshape(
        head_count, tok_rows, head_size
    )
    segment = lax.all_gather(w_out, "req", axis=1, tiled=True)
    shaped = segment.reshape(head_count, head_size, segment.shape[1])
    head_terms = jnp.einsum("htd,hdn->tn", attended, shaped, preferred_element_type=jnp.float32)
    projected = lax.psum_scatter(head_terms, "head", scatter_dimension=0, tiled=True).astype(
        jnp.bfloat16
    )
    return projected


def solution(mesh):
    return jax.shard_map(
        local,
        mesh=mesh,
        in_specs=(
            P(("groups", "req"), "head", None),
            P(("groups", "req"), "head", None),
            P(("groups", "req"), "head", None),
            P(("groups", "req"), "head", None, None, None),
            P("groups"),
            P("groups", None),
            P("groups", "head", None),
            P("head", "req"),
        ),
        out_specs=P(("groups", "req", "head"), None),
        check_vma=False,
    )
```

profile of v0, /device:TPU:0, one launch (start us, length us, event | category | flops | bytes accessed | tf_op | source)
XLA Modules:
  0.0 353.1 jit_solution(10308188675530318257)
XLA Ops:
  6.5 0.7 all-gather.2.cloned.1.call-update
  7.3 0.7 broadcast_compare_fusion
  8.0 0.5 convert_reduce_fusion
  8.5 0.7 add_select_fusion
  9.2 0.1 select_reduce_fusion
  9.3 0.1 copy.24
  9.4 0.7 compare_select_fusion.1
  10.1 0.1 copy.23
  10.2 0.1 reshape.176
  10.3 0.6 gather_fusion.3
  10.8 0.1 reshape.184
  11.0 5.2 %gather_fusion.4 = bf16[64,2,128,128]{3,2,1,0:T(8,128)(2,1)} fusion(bf16[64,2,128,128]{3,2,1,0:T(8,128)(2,1)} %bitcast.67, s32[1024]{0:T(1024)S(1)} %pad_clamp_fusion.1), kind=kCustom, calls=%fused_computation.4 | custom fusion | bytes 8388864 | tf_op jit(solution)/shard_map/gather | solution.py:32
  16.2 5.0 %copy.25 = bf16[8,2,4,2,128,128]{5,4,2,1,3,0:T(8,128)(2,1)} copy(bf16[8,2,4,2,128,128]{5,4,3,2,1,0:T(8,128)(2,1)} %bitcast.64) | data formatting | bytes 8388608 | tf_op jit(solution)/shard_map/gather | solution.py:32
  21.2 7.4 %all-to-all-start = ((bf16[8,2,4,2,128,128]{5,4,2,1,3,0:T(8,128)(2,1)}), bf16[8,2,4,2,128,128]{5,4,2,1,3,0:T(8,128)(2,1)}, u32[]{:S(2)}, u32[]{:S(2)}) async-start(bf16[8,2,4,2,128,128]{5,4,2,1,3,0:T(8,128)(2,1)} %copy.25), calls=%async_computation | async-start | bytes 8388608 | tf_op jit(solution)/shard_map/all_to_all | solution.py:33
  28.7 0.2 dynamic-slice_reduce_fusion
  28.9 0.6 gather_fusion.1
  29.4 0.6 gather_fusion
  30.0 0.2 select_reduce_fusion.1
  30.3 0.1 copy.27
  30.4 0.6 gather_fusion.2
  31.0 179.1 %all-to-all-done = bf16[8,2,4,2,128,128]{5,4,2,1,3,0:T(8,128)(2,1)} async-done(((bf16[8,2,4,2,128,128]{5,4,2,1,3,0:T(8,128)(2,1)}), bf16[8,2,4,2,128,128]{5,4,2,1,3,0:T(8,128)(2,1)}, u32[]{:S(2)}, u32[]{:S(2)}) %all-to-all-start) | async-done | bytes 4194336 | tf_op jit(solution)/shard_map/all_to_all | solution.py:33
  210.1 4.0 %fusion.24 = (bf16[8,2,4,1,128,128]{5,4,2,1,3,0:T(8,128)(2,1)}, bf16[8,2,4,1,128,128]{5,4,2,1,3,0:T(8,128)(2,1)S(1)}) fusion(bf16[8,2,4,2,128,128]{5,4,2,1,3,0:T(8,128)(2,1)} %all-to-all-done), kind=kLoop, calls=%fused_computation.57 | loop fusion | bytes 8388608 | tf_op jit(solution)/shard_map/slice | solution.py:49
  214.2 113.6 %while.11 = (s32[]{:T(128)}, bf16[4,4,128,128]{3,2,1,0:T(8,128)(2,1)S(1)}, s32[4]{0:T(128)S(1)}, bf16[128,16,128]{2,1,0:T(8,128)(2,1)}, bf16[8192,128]{1,0:T(8,1...) while((s32[]{:T(128)}, ...), condition=%wide.region_8.9_spmd.clone, body=%wide.region_3.8_spmd.clone.sunk | while | flops 2227846144 | bytes 57293268 | solution.py:82
  214.2 0.6 dynamic_slice.19
  215.4 1.0 constant_dynamic-slice_fusion.2
  216.4 0.1 add_compare_fusion.2
  216.5 7.1 %fusion.55 = (f32[512]{0:T(512)S(1)}, f32[512,8192]{1,0:T(8,128)}) fusion(pred[8192]{0:T(1024)(128)(4,1)S(1)} %bitcast.69, bf16[512,128]{1,0:T(8,128)(2,1)S(1)} %bitcast.65, bf16[8192,128]{1,0:T(8,128)(2,1)S(1)} %get-tuple-element.269), kind=kOutput, calls=%fused_computation.9.clone.1 | convolution fusion | flops 1086324224 | bytes 19015680 | tf_op jit(solution)/shard_map/while/body/eval_jaxpr/dot_general | solution.py:62
  223.6 0.1 tile.20
  223.7 0.2 fusion.56
  223.9 0.1 fusion.59
  224.0 9.8 %fusion.58 = f32[512]{0:T(512)S(1)} fusion(f32[512,8192]{1,0:T(8,128)} %get-tuple-element.231, f32[512]{0:T(512)S(1)} %max.9, pred[8192]{0:T(1024)(128)(4,1)S(1)} %bitcast.70), kind=kLoop, calls=%fused_computation.10.clone.1 | loop fusion | flops 16776704 | bytes 16789504 | tf_op jit(solution)/shard_map/while/body/eval_jaxpr/reduce_sum | solution.py:72
  233.8 8.4 %fusion.57 = f32[512,128]{1,0:T(8,128)S(1)} fusion(bf16[8192,128]{1,0:T(8,128)(2,1)} %get-tuple-element.271, f32[512,8192]{1,0:T(8,128)} %get-tuple-element.231, f32[512]{0:T(512)S(1)} %max.9, pred[8192]{0:T(1024)(128)(4,1)S(1)} %bitcast.71), kind=kOutput, calls=%fused_computation.12.clone.1 | convolution fusion | flops 1090519040 | bytes 19146752 | tf_op jit(solution)/shard_map/while/body/eval_jaxpr/dot_general | solution.py:73
  242.2 0.2 fusion.60
  242.5 0.6 dynamic_slice.19
  243.6 1.0 constant_dynamic-slice_fusion.2
  244.7 0.1 add_compare_fusion.2
  244.8 7.1 %fusion.55 = (f32[512]{0:T(512)S(1)}, f32[512,8192]{1,0:T(8,128)}) fusion(pred[8192]{0:T(1024)(128)(4,1)S(1)} %bitcast.69, bf16[512,128]{1,0:T(8,128)(2,1)S(1)} %bitcast.65, bf16[8192,128]{1,0:T(8,128)(2,1)S(1)} %get-tuple-element.269), kind=kOutput, calls=%fused_computation.9.clone.1 | convolution fusion | flops 1086324224 | bytes 19015680 | tf_op jit(solution)/shard_map/while/body/eval_jaxpr/dot_general | solution.py:62
  251.9 0.2 fusion.56
  252.2 0.1 fusion.59
  252.2 9.9 %fusion.58 = f32[512]{0:T(512)S(1)} fusion(f32[512,8192]{1,0:T(8,128)} %get-tuple-element.231, f32[512]{0:T(512)S(1)} %max.9, pred[8192]{0:T(1024)(128)(4,1)S(1)} %bitcast.70), kind=kLoop, calls=%fused_computation.10.clone.1 | loop fusion | flops 16776704 | bytes 16789504 | tf_op jit(solution)/shard_map/while/body/eval_jaxpr/reduce_sum | solution.py:72
  262.2 8.4 %fusion.57 = f32[512,128]{1,0:T(8,128)S(1)} fusion(bf16[8192,128]{1,0:T(8,128)(2,1)} %get-tuple-element.271, f32[512,8192]{1,0:T(8,128)} %get-tuple-element.231, f32[512]{0:T(512)S(1)} %max.9, pred[8192]{0:T(1024)(128)(4,1)S(1)} %bitcast.71), kind=kOutput, calls=%fused_computation.12.clone.1 | convolution fusion | flops 1090519040 | bytes 19146752 | tf_op jit(solution)/shard_map/while/body/eval_jaxpr/dot_general | solution.py:73
  270.6 0.2 fusion.60
  270.9 0.6 dynamic_slice.19
  272.1 1.0 constant_dynamic-slice_fusion.2
  273.1 0.1 add_compare_fusion.2
  273.2 7.3 %fusion.55 = (f32[512]{0:T(512)S(1)}, f32[512,8192]{1,0:T(8,128)}) fusion(pred[8192]{0:T(1024)(128)(4,1)S(1)} %bitcast.69, bf16[512,128]{1,0:T(8,128)(2,1)S(1)} %bitcast.65, bf16[8192,128]{1,0:T(8,128)(2,1)S(1)} %get-tuple-element.269), kind=kOutput, calls=%fused_computation.9.clone.1 | convolution fusion | flops 1086324224 | bytes 19015680 | tf_op jit(solution)/shard_map/while/body/eval_jaxpr/dot_general | solution.py:62
  280.6 0.2 fusion.56
  280.9 0.1 fusion.59
  280.9 9.9 %fusion.58 = f32[512]{0:T(512)S(1)} fusion(f32[512,8192]{1,0:T(8,128)} %get-tuple-element.231, f32[512]{0:T(512)S(1)} %max.9, pred[8192]{0:T(1024)(128)(4,1)S(1)} %bitcast.70), kind=kLoop, calls=%fused_computation.10.clone.1 | loop fusion | flops 16776704 | bytes 16789504 | tf_op jit(solution)/shard_map/while/body/eval_jaxpr/reduce_sum | solution.py:72
  290.9 8.4 %fusion.57 = f32[512,128]{1,0:T(8,128)S(1)} fusion(bf16[8192,128]{1,0:T(8,128)(2,1)} %get-tuple-element.271, f32[512,8192]{1,0:T(8,128)} %get-tuple-element.231, f32[512]{0:T(512)S(1)} %max.9, pred[8192]{0:T(1024)(128)(4,1)S(1)} %bitcast.71), kind=kOutput, calls=%fused_computation.12.clone.1 | convolution fusion | flops 1090519040 | bytes 19146752 | tf_op jit(solution)/shard_map/while/body/eval_jaxpr/dot_general | solution.py:73
  299.3 0.2 fusion.60
  299.6 0.6 dynamic_slice.19
  300.7 1.0 constant_dynamic-slice_fusion.2
  301.8 0.1 add_compare_fusion.2
  301.9 7.1 %fusion.55 = (f32[512]{0:T(512)S(1)}, f32[512,8192]{1,0:T(8,128)}) fusion(pred[8192]{0:T(1024)(128)(4,1)S(1)} %bitcast.69, bf16[512,128]{1,0:T(8,128)(2,1)S(1)} %bitcast.65, bf16[8192,128]{1,0:T(8,128)(2,1)S(1)} %get-tuple-element.269), kind=kOutput, calls=%fused_computation.9.clone.1 | convolution fusion | flops 1086324224 | bytes 19015680 | tf_op jit(solution)/shard_map/while/body/eval_jaxpr/dot_general | solution.py:62
  309.0 0.1 tile.20
  309.0 0.2 fusion.56
  309.3 0.1 fusion.59
  309.3 9.8 %fusion.58 = f32[512]{0:T(512)S(1)} fusion(f32[512,8192]{1,0:T(8,128)} %get-tuple-element.231, f32[512]{0:T(512)S(1)} %max.9, pred[8192]{0:T(1024)(128)(4,1)S(1)} %bitcast.70), kind=kLoop, calls=%fused_computation.10.clone.1 | loop fusion | flops 16776704 | bytes 16789504 | tf_op jit(solution)/shard_map/while/body/eval_jaxpr/reduce_sum | solution.py:72
  319.1 8.4 %fusion.57 = f32[512,128]{1,0:T(8,128)S(1)} fusion(bf16[8192,128]{1,0:T(8,128)(2,1)} %get-tuple-element.271, f32[512,8192]{1,0:T(8,128)} %get-tuple-element.231, f32[512]{0:T(512)S(1)} %max.9, pred[8192]{0:T(1024)(128)(4,1)S(1)} %bitcast.71), kind=kOutput, calls=%fused_computation.12.clone.1 | convolution fusion | flops 1090519040 | bytes 19146752 | tf_op jit(solution)/shard_map/while/body/eval_jaxpr/dot_general | solution.py:73
  327.6 0.2 fusion.60
  327.9 8.5 %convolution_bitcast_fusion = f32[128,4096]{1,0:T(8,128)} fusion(bf16[16,128,128]{2,1,0:T(8,128)(2,1)S(1)} %bitcast.74, bf16[16,128,4096]{2,1,0:T(8,128)(2,1)} %bitcast.63), kind=kOutput, calls=%fused_computation.28 | convolution fusion | flops 2147483648 | bytes 19398656 | tf_op jit(solution)/shard_map/htd,hdn->tn/dot_general | solution.py:87
  336.4 7.8 %reduce-scatter.2.cloned.1.call-done = f32[64,4096]{1,0:T(8,128)} async-done(((f32[128,4096]{1,0:T(8,128)}), f32[64,4096]{1,0:T(8,128)}) %reduce-scatter.2.cloned.1.call-update) | async-done | bytes 1048592 | tf_op jit(solution)/shard_map/reduce_scatter | solution.py:88
  344.2 2.1 convert_element_type.18
  (42 shorter events, 0.5 us)
Async XLA Ops:
  6.5 23.8 %copy-start = (s32[16]{0:T(128)S(1)}, s32[16]{0:T(128)}, u32[]{:S(2)}) copy-start(s32[16]{0:T(128)} %param.14) | copy-start | bytes 196
  6.5 22.1 %copy-start.1 = (s32[8,1,2]{0,2,1:T(2,128)S(1)}, s32[8,1,2]{0,2,1:T(2,128)}, u32[]{:S(2)}) copy-start(s32[8,1,2]{0,2,1:T(2,128)} %param.16) | copy-start | bytes 196
  6.5 321.3 %all-gather.2.cloned.1.call-start = ((), (), s32[]{:S(2)}) async-start(), calls=%async_computation.2 | async-start | bytes 18874368 | tf_op jit(solution)/shard_map/all_gather | solution.py:85
  10.9 203.2 %copy-start.2 = (bf16[128,1,128]{2,0,1:T(8,128)(2,1)S(1)}, bf16[128,1,128]{2,0,1:T(8,128)(2,1)}, u32[]{:S(2)}) copy-start(bf16[128,1,128]{2,0,1:T(8,128)(2,1)} %param.11) | copy-start | bytes 98308
  11.0 203.2 %copy-start.3 = (bf16[128,1,128]{2,0,1:T(8,128)(2,1)S(1)}, bf16[128,1,128]{2,0,1:T(8,128)(2,1)}, u32[]{:S(2)}) copy-start(bf16[128,1,128]{2,0,1:T(8,128)(2,1)} %param.12) | copy-start | bytes 98308
  21.2 188.9 %all-to-all-start = ((bf16[8,2,4,2,128,128]{5,4,2,1,3,0:T(8,128)(2,1)}), bf16[8,2,4,2,128,128]{5,4,2,1,3,0:T(8,128)(2,1)}, u32[]{:S(2)}, u32[]{:S(2)}) async-start(bf16[8,2,4,2,128,128]{5,4,2,1,3,0:T(8,128)(2,1)} %copy.25), calls=%async_computation | async-start | bytes 8388608 | tf_op jit(solution)/shard_map/all_to_all | solution.py:33
  28.6 315.6 %reduce-scatter.2.cloned.1.call-start = ((), (), s32[]{:S(2)}) async-start(), calls=%async_computation.3 | async-start | bytes 3145728 | tf_op jit(solution)/shard_map/reduce_scatter | solution.py:88
Sparse Core Ops, SparseCore 0:
  9.4 311.4 all-gather.1
  336.5 7.6 reduce-scatter.1
where the time goes:
time: 354 us; the launch traced here: 353 us
  waiting for transfers between devices  188 us (53%)
  matrix products  72.6 us (21%)
  other arithmetic  45.2 us (13%)
  local copies, waits for them, and re-layouts  24.1 us (7%)
  between operations  13.5 us (4%)
  starting transfers between devices  7.45 us (2%)
    all_to_all x1, waiting for transfers between devices, local(): lax.all_to_all(outgoing, 'req', split_axis=0, concat_axis=0, tiled=True)  179 us
    reduce_sum x8, other arithmetic, one_block(): row_total = jnp.sum(cached_weights, axis=1) + jnp.sum(own_weights, axis=1)  39.7 us
    dot_general x4, matrix products, one_block(): jnp.dot(cached_weights.astype(jnp.bfloat16), cached_values, preferred_ele...  33.7 us
    dot_general x4, matrix products, one_block(): jnp.dot(query_rows, cached_keys.T, preferred_element_type=jnp.float32)  28.6 us
    gather x2, local copies, waits for them, and re-layouts, local(): outgoing = cluster_kv[:, 0][send_slots]  10.2 us
    dot_general x1, matrix products, local(): jnp.einsum('htd,hdn->tn', attended, shaped, preferred_element_type=jnp.fl...  8.51 us
    reduce_scatter x1, waiting for transfers between devices, local(): lax.psum_scatter(head_terms, 'head', scatter_dimension=0, tiled=True)  7.81 us
    all_to_all x1, starting transfers between devices, local(): lax.all_to_all(outgoing, 'req', split_axis=0, concat_axis=0, tiled=True)  7.42 us
  transfers between devices with their start and end apart: 3, of which 2 were waited for; matrix products, arithmetic and copies ran while one was open for 37% of the time, Pallas kernels for 0%

commit v1 on v0

v1 whole, which is shorter than its diff:
```python
import functools
import math

import jax
import jax.numpy as jnp
from jax import lax
from jax.experimental import pallas as pl
from jax.experimental.pallas import tpu as pltpu
from jax.sharding import PartitionSpec as P

LOW = -1e30
VMEM_LIMIT = 48 * 1024 * 1024


def swap(array, axis, size, mask):
    return lax.ppermute(array, axis, [(i, i ^ mask) for i in range(size)])


def pack_kernel(masks, partner, per_peer, slot_ref, ids_ref, kv_ref, *rest):
    outs, (table, sems) = rest[:-2], rest[-2:]
    me = lax.axis_index("req")
    clusters, pieces = slot_ref.shape
    held = kv_ref.shape[0]
    picks = ids_ref.shape[2]
    low = me * held

    def scan(c, carry):
        count = jnp.int32(0)
        for p in range(pieces):
            slot = slot_ref[c, p] - low
            table[c, count] = slot
            count = count + ((slot >= 0) & (slot < held)).astype(jnp.int32)
        return carry

    lax.fori_loop(0, clusters, scan, 0)
    copies = []
    for part in range(2):
        for index, mask in enumerate(masks):
            request = me ^ mask
            if part == 0:
                request = request ^ partner
            out = outs[part * len(masks) + index]
            for s in range(picks):
                c = ids_ref[request, 0, s]
                for k in range(per_peer):
                    copies.append(
                        pltpu.make_async_copy(
                            kv_ref.at[table[c, k], 0], out.at[s * per_peer + k], sems.at[len(copies)]
                        )
                    )
                    copies[-1].start()
    for copy in copies:
        copy.wait()


def pack(piece_slot, cluster_ids, cluster_kv, masks, partner, per_peer):
    picks = cluster_ids.shape[2]
    count = picks * per_peer
    shape = jax.ShapeDtypeStruct((count,) + cluster_kv.shape[2:], cluster_kv.dtype)
    smem = pl.BlockSpec(memory_space=pltpu.SMEM)
    anywhere = pl.BlockSpec(memory_space=pl.ANY)
    total = 2 * len(masks)
    size = total * count * math.prod(cluster_kv.shape[2:]) * 2
    return pl.pallas_call(
        functools.partial(pack_kernel, masks, partner, per_peer),
        out_shape=[shape] * total,
        in_specs=[smem, smem, anywhere],
        out_specs=[anywhere] * total,
        scratch_shapes=[
            pltpu.SMEM((piece_slot.shape[0], pieces_up(per_peer)), jnp.int32),
            pltpu.SemaphoreType.DMA((total * count,)),
        ],
        cost_estimate=pl.CostEstimate(flops=0, bytes_accessed=2 * size, transcendentals=0),
        name="pack_pieces",
    )(piece_slot, cluster_ids, cluster_kv)


def pieces_up(per_peer):
    return per_peer + 1


def attend_kernel(settings, *refs):
    own, heads, block, rows_step, picks, per_peer, sources, scale = settings
    if own:
        q_ref, valid_ref, slot_ref, pool_ref, own_k, own_v = refs[:6]
        rest = refs[6:]
    else:
        q_ref, valid_ref, slot_ref, pool_ref = refs[:4]
        rest = refs[4:]
    got = rest[: sources - 1]
    out_ref, stat_ref = rest[sources - 1 : sources + 1] if own else (rest[sources - 1], None)
    kv, bias, scores, tops, total, mixed, lse, sem = rest[sources + (1 if own else 0) :]
    rows, size = q_ref.shape
    keys = kv.shape[2]
    each = picks * per_peer
    lane = lax.broadcasted_iota(jnp.int32, (1, keys), 1)
    slots = kv.shape[0]

    at = jnp.int32(0)
    for j in range(sources):
        for e in range(each):
            valid = valid_ref[j, e]

            @pl.when(valid > 0)
            def _(j=j, e=e, valid=valid, at=at):
                source = pool_ref.at[slot_ref[e], 0] if j == 0 else got[j - 1].at[e]
                pltpu.make_async_copy(source, kv.at[at], sem).start()
                bias[at] = jnp.where(lane < valid, 0.0, LOW)

            at = at + (valid > 0).astype(jnp.int32)
    count = at
    blocks = (count + block - 1) // block

    @pl.when(count > 0)
    def _():
        for extra in range(block - 1):
            spot = count + extra

            @pl.when(spot < blocks * block)
            def _(spot=spot):
                pltpu.make_async_copy(pool_ref.at[0, 0], kv.at[spot], sem).start()
                bias[spot] = jnp.full((1, keys), LOW, jnp.float32)

    def wait(i, carry):
        pltpu.make_async_copy(pool_ref.at[0, 0], kv.at[0], sem).wait()
        return carry

    lax.fori_loop(0, blocks * block, wait, 0)

    def load(b, which):
        return kv[pl.ds(b * block, block), which].reshape(block * keys, size)

    def fold(values, op):
        parts = [values[:, i * keys : (i + 1) * keys] for i in range(values.shape[1] // keys)]
        while len(parts) > 1:
            parts = [op(parts[i], parts[i + 1]) if i + 1 < len(parts) else parts[i] for i in range(0, len(parts), 2)]
        return parts[0]

    def score(i, b):
        q = q_ref[pl.ds(i * rows_step, rows_step), :]
        s = lax.dot_general(q, load(b, 0), (((1,), (1,)), ((), ())), preferred_element_type=jnp.float32)
        line = bias[pl.ds(b * block, block)]
        s = s * scale + jnp.concatenate([line[n] for n in range(block)], axis=1)
        scores[i % 2, b] = s
        tops[i % 2] = jnp.maximum(tops[i % 2], fold(s, jnp.maximum))

    def start(i):
        if own:
            q = q_ref[pl.ds(i * rows_step, rows_step), :]
            s = lax.dot_general(q, own_k[...], (((1,), (1,)), ((), ())), preferred_element_type=jnp.float32)
            position = (lax.broadcasted_iota(jnp.int32, s.shape, 0) + i * rows_step) // heads
            s = jnp.where(position >= lax.broadcasted_iota(jnp.int32, s.shape, 1), s * scale, LOW)
            scores[i % 2, scores.shape[1] - 1, :, : s.shape[1]] = s
            tops[i % 2] = s
        else:
            tops[i % 2] = jnp.full(tops.shape[1:], LOW, jnp.float32)

    def weigh(i, b, top):
        p = jnp.exp2(scores[i % 2, b] - top)
        total[...] += fold(p, jnp.add)
        mixed[...] += jnp.dot(p.astype(jnp.bfloat16), load(b, 1), preferred_element_type=jnp.float32)

    steps = rows // rows_step
    eye = lax.broadcasted_iota(jnp.int32, (keys, keys), 0) == lax.broadcasted_iota(jnp.int32, (keys, keys), 1)
    for i in range(steps + 1):
        top = None
        if i > 0:
            top = jnp.max(tops[(i - 1) % 2], axis=1, keepdims=True)
            if own:
                p = jnp.exp2(scores[(i - 1) % 2, scores.shape[1] - 1, :, : own_k.shape[0]] - top)
                total[...] = p
                mixed[...] = jnp.dot(p.astype(jnp.bfloat16), own_v[...], preferred_element_type=jnp.float32)
            else:
                total[...] = jnp.zeros(total.shape, jnp.float32)
                mixed[...] = jnp.zeros(mixed.shape, jnp.float32)
        if i < steps:
            start(i)

        def body(b, carry, i=i, top=top):
            if i < steps:
                score(i, b)
            if i > 0:
                weigh(i - 1, b, top)
            return carry

        lax.fori_loop(0, blocks, body, 0)
        if i > 0:
            row_sum = jnp.sum(total[...], axis=1, keepdims=True)
            some = row_sum > 0.0
            safe = jnp.where(some, row_sum, 1.0)
            normal = mixed[...] / safe
            first = (i - 1) * rows_step
            out_ref[pl.ds(first, rows_step), :] = normal.astype(out_ref.dtype)
            log_sum = jnp.where(some, top + jnp.log2(safe), LOW)
            for n in range(rows_step // keys):
                column = log_sum[n * keys : (n + 1) * keys]
                line = jnp.sum(jnp.where(eye, column, 0.0), axis=0, keepdims=True)
                lse[pl.ds(first // keys + n, 1), :] = line
    if own:
        stat_ref[...] = lse[...]
    else:
        left = lse[...]
        lines = lse.shape[0]
        for n in range(3):
            part = left.astype(jnp.bfloat16)
            out_ref[pl.ds(rows + n * lines, lines), :] = part
            left = left - part.astype(jnp.float32)


def attend(q, valid, slots, pool, own_keys, own_values, got, heads):
    own = own_keys is not None
    rows, size = q.shape
    sources, each = valid.shape
    keys = pool.shape[3]
    block = 4
    rows_step = math.gcd(rows, 512)
    lines = rows // keys
    scale = size ** -0.5 * math.log2(math.e)
    picks = 1
    settings = (own, heads, block, rows_step, picks, each, sources, scale)
    smem = pl.BlockSpec(memory_space=pltpu.SMEM)
    vmem = pl.BlockSpec(memory_space=pltpu.VMEM)
    anywhere = pl.BlockSpec(memory_space=pl.ANY)
    most = -(-sources * each // block)
    if own:
        out_shape = [
            jax.ShapeDtypeStruct((rows, size), jnp.float32),
            jax.ShapeDtypeStruct((lines, keys), jnp.float32),
        ]
        operands = (q, valid, slots, pool, own_keys, own_values, *got)
        in_specs = [vmem, smem, smem, anywhere, vmem, vmem] + [anywhere] * len(got)
    else:
        out_shape = jax.ShapeDtypeStruct((rows + 3 * lines, size), jnp.bfloat16)
        operands = (q, valid, slots, pool, *got)
        in_specs = [vmem, smem, smem, anywhere] + [anywhere] * len(got)
    work = rows * sources * each * keys
    return pl.pallas_call(
        functools.partial(attend_kernel, settings),
        out_shape=out_shape,
        in_specs=in_specs,
        out_specs=[vmem, vmem] if own else vmem,
        scratch_shapes=[
            pltpu.VMEM((most * block,) + pool.shape[2:], pool.dtype),
            pltpu.VMEM((most * block, 1, keys), jnp.float32),
            pltpu.VMEM((2, most + (1 if own else 0), rows_step, block * keys), jnp.float32),
            pltpu.VMEM((2, rows_step, keys), jnp.float32),
            pltpu.VMEM((rows_step, keys), jnp.float32),
            pltpu.VMEM((rows_step, size), jnp.float32),
            pltpu.VMEM((lines, keys), jnp.float32),
            pltpu.SemaphoreType.DMA,
        ],
        compiler_params=pltpu.CompilerParams(vmem_limit_bytes=VMEM_LIMIT),
        cost_estimate=pl.CostEstimate(flops=8 * work * size, bytes_accessed=4 << 20, transcendentals=work),
        name="attend_own" if own else "attend_partner",
    )(*operands)


def combine_kernel(heads, out_mine, lse_mine, other, attended, scratch):
    rows, size = out_mine.shape
    lines, keys = lse_mine.shape
    eye = lax.broadcasted_iota(jnp.int32, (keys, keys), 0) == lax.broadcasted_iota(jnp.int32, (keys, keys), 1)
    mine = lse_mine[...]
    theirs = sum(other[pl.ds(rows + n * lines, lines), :].astype(jnp.float32) for n in range(3))
    top = jnp.maximum(mine, theirs)
    mine, theirs = jnp.exp2(mine - top), jnp.exp2(theirs - top)
    share = theirs / (mine + theirs)
    for n in range(lines):
        column = jnp.sum(jnp.where(eye, share[n : n + 1], 0.0), axis=1, keepdims=True)
        here = pl.ds(n * keys, keys)
        a = out_mine[here, :]
        scratch[here, :] = a + column * (other[here, :].astype(jnp.float32) - a)
    tokens = rows // heads
    for h in range(heads):
        attended[:, h * size : (h + 1) * size] = scratch[pl.ds(h, tokens, stride=heads), :].astype(attended.dtype)


def combine(out_mine, lse_mine, other, heads):
    rows, size = out_mine.shape
    vmem = pl.BlockSpec(memory_space=pltpu.VMEM)
    return pl.pallas_call(
        functools.partial(combine_kernel, heads),
        out_shape=jax.ShapeDtypeStruct((rows // heads, heads * size), jnp.bfloat16),
        in_specs=[vmem] * 3,
        out_specs=vmem,
        scratch_shapes=[pltpu.VMEM((rows, size), jnp.float32)],
        compiler_params=pltpu.CompilerParams(vmem_limit_bytes=VMEM_LIMIT),
        cost_estimate=pl.CostEstimate(flops=4 * rows * size, bytes_accessed=8 * rows * size, transcendentals=0),
        name="combine",
    )(out_mine, lse_mine, other)


def place_kernel(masks, *refs):
    parts, (out, sems) = refs[:-2], refs[-2:]
    me = lax.axis_index("req")
    width = parts[0].shape[2]
    copies = []
    for part, mask in zip(parts, masks):
        for side in range(2):
            column = ((me ^ mask) ^ side) * width
            copies.append(
                pltpu.make_async_copy(
                    part.at[side], out.at[:, pl.ds(pl.multiple_of(column, 128), width)], sems.at[len(copies)]
                )
            )
            copies[-1].start()
    for copy in copies:
        copy.wait()


def place(parts, masks):
    _, rows, width = parts[0].shape
    anywhere = pl.BlockSpec(memory_space=pl.ANY)
    return pl.pallas_call(
        functools.partial(place_kernel, masks),
        out_shape=jax.ShapeDtypeStruct((rows, 2 * len(parts) * width), parts[0].dtype),
        in_specs=[anywhere] * len(parts),
        out_specs=anywhere,
        scratch_shapes=[pltpu.SemaphoreType.DMA((2 * len(parts),))],
        name="place_columns",
    )(*parts)


def local(queries, new_keys, new_values, cluster_kv, cluster_len, piece_slot, cluster_ids, w_out):
    me = lax.axis_index("req")
    core = lax.axis_index("head")
    peers = lax.axis_size("req")
    cores = lax.axis_size("head")
    tokens, heads, size = queries.shape
    held = cluster_kv.shape[0]
    keys = cluster_kv.shape[3]
    pieces = piece_slot.shape[1]
    per_peer = pieces // peers
    half = peers // 2
    masks = list(range(1, half))

    packed = pack(piece_slot, cluster_ids, cluster_kv, masks, half, per_peer)
    q_mine = queries.reshape(tokens * heads, size)
    q_theirs = swap(q_mine, "req", peers, half)
    got_theirs = [swap(a, "req", peers, m) for a, m in zip(packed[: len(masks)], masks)]

    owner = piece_slot // held
    position = jnp.arange(pieces, dtype=jnp.int32)
    same = (owner[:, :, None] == owner[:, None, :]) & (position[:, None] > position[None, :])[None]
    rank = jnp.sum(same.astype(jnp.int32), axis=2)

    def tables(request):
        chosen = lax.dynamic_index_in_dim(cluster_ids, request, 0, keepdims=False)[0]
        own_owner, own_rank, own_slot = owner[chosen], rank[chosen], piece_slot[chosen] % held
        sender = me ^ jnp.arange(half, dtype=jnp.int32)
        fits = (own_owner[None, :, None, :] == sender[:, None, None, None]) & (
            own_rank[None, :, None, :] == jnp.arange(per_peer, dtype=jnp.int32)[None, None, :, None]
        )
        filled = jnp.clip(cluster_len[chosen][:, None] - position[None, :] * keys, 0, keys)
        valid = jnp.sum(jnp.where(fits, filled[None, :, None, :], 0), axis=3).reshape(half, -1)
        slots = jnp.sum(jnp.where(fits[0], own_slot[:, None, :], 0), axis=2).reshape(-1)
        return valid, slots

    valid_theirs, slots_theirs = tables(me ^ half)
    valid_mine, slots_mine = tables(me)

    part = attend(q_theirs, valid_theirs, slots_theirs, cluster_kv, None, None, got_theirs, heads)
    later = lax.optimization_barrier((tuple(packed[len(masks) :]), tuple(got_theirs)))[0]
    got_mine = [swap(a, "req", peers, m) for a, m in zip(later, masks)]
    part = swap(part, "req", peers, half)
    w_later = lax.optimization_barrier((w_out, tuple(got_mine)))[0]
    w_pair = swap(w_later, "req", peers, 1)
    mine, lse = attend(
        q_mine, valid_mine, slots_mine, cluster_kv, new_keys[:, 0], new_values[:, 0], got_mine, heads
    )
    attended = combine(mine, lse, part, heads)

    have = {0: attended}
    bit = half
    while bit > 1:
        for mask in list(have):
            have[mask ^ bit] = swap(have[mask], "req", peers, bit)
        bit //= 2

    share = tokens // cores
    results = {}
    for mask, rows in have.items():
        def product(which, rows=rows):
            few = lax.dynamic_slice_in_dim(rows, which * share, share, 0)
            return [jnp.dot(few, w, preferred_element_type=jnp.float32) for w in (w_out, w_pair)]

        away = jnp.stack([a.astype(jnp.bfloat16) for a in product(core ^ 1)])
        away = swap(away, "head", cores, 1)
        summed = (jnp.stack(product(core)) + away.astype(jnp.float32)).astype(jnp.bfloat16)
        results[mask] = swap(summed, "req", peers, mask) if mask else summed
    return place(list(results.values()), list(results))


def solution(mesh):
    return jax.shard_map(
        local,
        mesh=mesh,
        in_specs=(
            P(("groups", "req"), "head", None),
            P(("groups", "req"), "head", None),
            P(("groups", "req"), "head", None),
            P(("groups", "req"), "head", None, None, None),
            P("groups"),
            P("groups", None),
            P("groups", "head", None),
            P("head", "req"),
        ),
        out_specs=P(("groups", "req", "head"), None),
        check_vma=False,
    )
```

time: 354 us -> 271 us (0.77)
  Pallas kernels: 0 us -> 147 us
  waiting for transfers between devices: 188 us -> 56.1 us
  matrix products: 72.6 us -> 22.4 us
  other arithmetic: 45.2 us -> 2.16 us
  starting transfers between devices: 7.45 us -> 32.6 us
  local copies, waits for them, and re-layouts: 24.1 us -> 7.85 us
  between operations: 13.5 us -> 0.57 us
    all_to_all x1 -> x0, waiting for transfers between devices: 179 us -> none  [local(): lax.all_to_all(outgoing, 'req', split_axis=0, concat_axis=0, tiled=True)]
    pallas_call x0 -> x5, Pallas kernels: none -> 147 us  [the longest x1 100 us: pack(): pl.pallas_call(functools.partial(pack_kernel, masks, partner, per_peer),...]
    ppermute x0 -> x19, waiting for transfers between devices: none -> 56.1 us  [swap(): return lax.ppermute(array, axis, [(i, i ^ mask) for i in range(size)])]
    dot_general x17 -> x16, matrix products: 72.6 us -> 22.4 us  [product(): jnp.dot(few, w, preferred_element_type=jnp.float32)]
    reduce_sum x11 -> x4, other arithmetic: 40.5 us -> 1.12 us  [the longest x1 0.45 us: local(): rank = jnp.sum(same.astype(jnp.int32), axis=2)]
    ppermute x0 -> x19, starting transfers between devices: none -> 32.6 us  [swap(): return lax.ppermute(array, axis, [(i, i ^ mask) for i in range(size)])]
    gather x6 -> x8, local copies, waits for them, and re-layouts: 12.5 us -> 4.63 us  [the longest x2 1.28 us: tables(): cluster_len[chosen][:, None] - position[None, :] * keys]
    reduce_scatter x1 -> x0, waiting for transfers between devices: 7.81 us -> none  [local(): lax.psum_scatter(head_terms, 'head', scatter_dimension=0, tiled=True)]
  transfers between devices with their start and end apart: 3 -> 19, of which waited for: 2 -> 9; matrix products, arithmetic and copies ran while one was open for 37% -> 11% of each run, Pallas kernels for 0% -> 11%
where the time goes in v1:
time: 271 us; the launch traced here: 269 us
  Pallas kernels  147 us (54%)
  waiting for transfers between devices  56.1 us (21%)
  starting transfers between devices  32.6 us (12%)
  matrix products  22.4 us (8%)
  local copies, waits for them, and re-layouts  7.85 us (3%)
    pallas_call x1, Pallas kernels, pack(): pl.pallas_call(functools.partial(pack_kernel, masks, partner, per_peer),...  100 us
    ppermute x19, waiting for transfers between devices, swap(): return lax.ppermute(array, axis, [(i, i ^ mask) for i in range(size)])  56.1 us
    ppermute x19, starting transfers between devices, swap(): return lax.ppermute(array, axis, [(i, i ^ mask) for i in range(size)])  32.6 us
    pallas_call x2, Pallas kernels, attend(): pl.pallas_call(functools.partial(attend_kernel, settings), out_shape=out_...  29.5 us
    dot_general x16, matrix products, product(): jnp.dot(few, w, preferred_element_type=jnp.float32)  22.4 us
    pallas_call x1, Pallas kernels, place(): pl.pallas_call(functools.partial(place_kernel, masks), out_shape=jax.Shap...  17.1 us
  transfers between devices with their start and end apart: 19, of which 9 were waited for; matrix products, arithmetic and copies ran while one was open for 11% of the time, Pallas kernels for 11%

profile of v1, /device:TPU:0, one launch (start us, length us, event | category | flops | bytes accessed | tf_op | source)
XLA Modules:
  0.0 268.9 jit_solution(3979804347973088813)
XLA Ops:
  0.0 1.4 copy.11.ids_ref
  1.4 100.0 %pack_pieces.1 = (bf16[8,2,128,128]{3,2,1,0:T(8,128)(2,1)}, bf16[8,2,128,128]{3,2,1,0:T(8,128)(2,1)}, bf16[8,2,128,128]{3,2,1,0:T(8,128)(2,1)}, bf16[8,2,128,128...) custom-call(s32[16,32]{1,0:T(8,128)} %slot_ref.1, s32[8,1,2]{2,1,0:T(1,128)} %copy.11.ids_ref, ...), custom_call_target="tpu_custom_call" | custom-call | bytes 6291456 | tf_op jit(solution)/shard_map/pack_pieces/pallas_call | solution.py:64
  101.4 3.0 %collective-permute-start = (bf16[8,2,128,128]{3,2,1,0:T(8,128)(2,1)}, bf16[8,2,128,128]{3,2,1,0:T(8,128)(2,1)S(1)}, u32[]{:S(2)}, u32[]{:S(2)}) collective-permute-start(bf16[8,2,128,128]{3,2,1,0:T(8,128)(2,1)} %get-tuple-element.20), channel_id=1, source_target_pairs={{0,2},{2,0},{4,6},{6,4},{8,10},{10,8},{12,14},{14,12},{1,3},{3,1},... | collective-permute-start | bytes 1572872 | tf_op jit(solution)/shard_map/ppermute | solution.py:16
  104.4 1.6 collective-permute-start.1
  106.0 3.0 %collective-permute-start.6 = (bf16[2048,128]{1,0:T(8,128)(2,1)S(1)}, bf16[2048,128]{1,0:T(8,128)(2,1)S(1)}, u32[]{:S(2)}, u32[]{:S(2)}) collective-permute-start(bf16[2048,128]{1,0:T(8,128)(2,1)S(1)} %bitcast.67), channel_id=1, source_target_pairs={{0,8},{2,10},{4,12},{6,14},{8,0},{10,2},{12,4},{14,6},{1,9},{3,11}... | collective-permute-start | bytes 1572872 | tf_op jit(solution)/shard_map/ppermute | solution.py:16
  109.0 0.2 fusion.49
  109.3 0.6 gather_fusion
  109.9 0.6 gather_fusion.4
  110.4 0.6 gather_fusion.2
  111.1 0.6 gather_fusion.6
  111.7 0.5 convert_reduce_fusion
  112.2 0.6 gather_fusion.5
  112.8 0.6 gather_fusion.1
  113.3 0.6 gather_fusion.3
  113.9 0.6 gather_fusion.7
  114.5 0.1 broadcast_compare_fusion
  114.6 0.4 select_reduce_fusion
  115.0 0.1 select_reduce_fusion.2
  115.1 0.1 reshape.208.refs_2_
  115.2 0.1 reshape.207.refs_1_
  115.3 0.2 select_reduce_fusion.3
  115.4 0.1 reshape.206.refs_2_
  115.5 0.1 reshape.205.refs_1_
  115.6 1.0 collective-permute-done.refs_4_
  116.6 14.2 %collective-permute-done.1.refs_5_ = bf16[8,2,128,128]{3,2,1,0:T(8,128)(2,1)S(1)} collective-permute-done((bf16[8,2,128,128]{3,2,1,0:T(8,128)(2,1)}, bf16[8,2,128,128]{3,2,1,0:T(8,128)(2,1)S(1)}, u32[]{:S(2)}, u32[]{:S(2)}) %collective-permute-start.1) | collective-permute-done | bytes 524320 | tf_op jit(solution)/shard_map/ppermute | solution.py:16
  130.7 9.6 %collective-permute-done.2.refs_6_ = bf16[8,2,128,128]{3,2,1,0:T(8,128)(2,1)S(1)} collective-permute-done((bf16[8,2,128,128]{3,2,1,0:T(8,128)(2,1)}, bf16[8,2,128,128]{3,2,1,0:T(8,128)(2,1)S(1)}, u32[]{:S(2)}, u32[]{:S(2)}) %collective-permute-start.2) | collective-permute-done | bytes 524320 | tf_op jit(solution)/shard_map/ppermute | solution.py:16
  140.3 1.7 collective-permute-start.3
  142.0 1.8 collective-permute-start.5
  143.8 12.1 %attend_partner.1 = bf16[2096,128]{1,0:T(8,128)(2,1)S(1)} custom-call(bf16[2048,128]{1,0:T(8,128)(2,1)S(1)} %collective-permute-done.6.refs_0_, s32[4,8]{1,0:T(4,128)S(1)} %reshape.207.refs_1_, s32[8]{0:T(128)S(1)} %reshape.208.refs_2_, bf16[64,1,2,128,128]{4,3,2,1,0:T(8,128)(2,1)} %refs_3_.3, bf16[8,2,128,128]{3,2,1,0:T(8,128)(2,1)S(1)} %collective-permute-done.refs_4_, ...), custom_call_target="tpu_custom_call" | custom-call | flops 8589934592 | bytes 4194304 | tf_op jit(solution)/shard_map/attend_partner/pallas_call | solution.py:237
  155.9 7.1 %collective-permute-start.7 = (bf16[2096,128]{1,0:T(8,128)(2,1)S(1)}, bf16[2096,128]{1,0:T(8,128)(2,1)S(1)}, u32[]{:S(2)}, u32[]{:S(2)}) collective-permute-start(bf16[2096,128]{1,0:T(8,128)(2,1)S(1)} %attend_partner.1), channel_id=1, source_target_pairs={{0,8},{2,10},{4,12},{6,14},{8,0},{10,2},{12,4},{14,6},{1,9},{3,11}... | collective-permute-start | bytes 1609736 | tf_op jit(solution)/shard_map/ppermute | solution.py:16
  163.0 8.5 %collective-permute-done.5.refs_8_ = bf16[8,2,128,128]{3,2,1,0:T(8,128)(2,1)S(1)} collective-permute-done((bf16[8,2,128,128]{3,2,1,0:T(8,128)(2,1)}, bf16[8,2,128,128]{3,2,1,0:T(8,128)(2,1)S(1)}, u32[]{:S(2)}, u32[]{:S(2)}) %collective-permute-start.5) | collective-permute-done | bytes 524320 | tf_op jit(solution)/shard_map/ppermute | solution.py:16
  171.6 17.4 %attend_own.1 = (f32[2048,128]{1,0:T(8,128)S(1)}, f32[16,128]{1,0:T(8,128)S(1)}) custom-call(bf16[2048,128]{1,0:T(8,128)(2,1)S(1)} %bitcast.68, s32[4,8]{1,0:T(4,128)S(1)} %reshape.205.refs_1_, s32[8]{0:T(128)S(1)} %reshape.206.refs_2_, bf16[64,1,2,128,128]{4,3,2,1,0:T(8,128)(2,1)} %refs_3_.3, bf16[128,128]{1,0:T(8,128)(2,1)S(1)} %bitcast.69, ...), custom_call_target="tpu_custom_call" | custom-call | flops 8589934592 | bytes 4194304 | tf_op jit(solution)/shard_map/attend_own/pallas_call | solution.py:237
  189.0 0.6 combine.1
  189.7 8.4 %collective-permute-start.13 = (bf16[128,2048]{1,0:T(8,128)(2,1)S(1)}, bf16[128,2048]{1,0:T(8,128)(2,1)}, u32[]{:S(2)}, u32[]{:S(2)}) collective-permute-start(bf16[128,2048]{1,0:T(8,128)(2,1)S(1)} %combine.1), channel_id=1, source_target_pairs={{0,4},{2,6},{4,0},{6,2},{8,12},{10,14},{12,8},{14,10},{1,5},{3,7},... | collective-permute-start | bytes 1572872 | tf_op jit(solution)/shard_map/ppermute | solution.py:16
  198.1 2.1 fusion
  200.2 2.1 convolution_bitcast_fusion.7
  202.3 8.2 %collective-permute-done.10 = bf16[128,2048]{1,0:T(8,128)(2,1)S(1)} collective-permute-done((bf16[128,2048]{1,0:T(8,128)(2,1)S(1)}, bf16[128,2048]{1,0:T(8,128)(2,1)S(1)}, u32[]{:S(2)}, u32[]{:S(2)}) %collective-permute-start.10) | collective-permute-done | bytes 524320 | tf_op jit(solution)/shard_map/ppermute | solution.py:16
  210.5 0.1 collective-permute-start.16
  210.6 6.4 %collective-permute-done.13 = bf16[128,2048]{1,0:T(8,128)(2,1)} collective-permute-done((bf16[128,2048]{1,0:T(8,128)(2,1)S(1)}, bf16[128,2048]{1,0:T(8,128)(2,1)}, u32[]{:S(2)}, u32[]{:S(2)}) %collective-permute-start.13) | collective-permute-done | bytes 524320 | tf_op jit(solution)/shard_map/ppermute | solution.py:16
  217.0 2.2 fusion.4
  219.1 2.2 convolution_bitcast_fusion.3
  221.3 2.1 fusion.2
  223.4 2.1 convolution_bitcast_fusion.5
  225.5 2.3 collective-permute-done.16
  227.8 2.1 fusion.6
  229.9 2.1 convolution_bitcast_fusion.1
  232.0 0.5 fusion.7
  232.6 1.4 fusion.5
  234.0 0.6 collective-permute-start.14
  234.6 0.5 fusion.3
  235.1 0.1 collective-permute-start.11
  235.2 0.5 fusion.1
  235.7 0.6 collective-permute-start.9
  236.2 0.5 convolution_bitcast_fusion
  236.7 1.4 convolution_bitcast_fusion.2
  238.1 0.5 convolution_bitcast_fusion.4
  238.6 0.5 convolution_bitcast_fusion.6
  239.4 4.4 %collective-permute-start.12 = (bf16[2,64,512]{2,1,0:T(8,128)(2,1)S(1)}, bf16[2,64,512]{2,1,0:T(8,128)(2,1)S(1)}, u32[]{:S(2)}, u32[]{:S(2)}) collective-permute-start(bf16[2,64,512]{2,1,0:T(8,128)(2,1)S(1)} %fusion.9), channel_id=1, source_target_pairs={{0,8},{2,10},{4,12},{6,14},{8,0},{10,2},{12,4},{14,6},{1,9},{3,11}... | collective-permute-start | bytes 393224 | tf_op jit(solution)/shard_map/ppermute | solution.py:16
  243.8 0.7 fusion.8.refs_0_
  244.5 3.0 %collective-permute-done.18.refs_3_ = bf16[2,64,512]{2,1,0:T(8,128)(2,1)S(1)} collective-permute-done((bf16[2,64,512]{2,1,0:T(8,128)(2,1)S(1)}, bf16[2,64,512]{2,1,0:T(8,128)(2,1)S(1)}, u32[]{:S(2)}, u32[]{:S(2)}) %collective-permute-start.18) | collective-permute-done | bytes 131104 | tf_op jit(solution)/shard_map/ppermute | solution.py:16
  247.5 2.9 %collective-permute-done.15.refs_2_ = bf16[2,64,512]{2,1,0:T(8,128)(2,1)S(1)} collective-permute-done((bf16[2,64,512]{2,1,0:T(8,128)(2,1)S(1)}, bf16[2,64,512]{2,1,0:T(8,128)(2,1)S(1)}, u32[]{:S(2)}, u32[]{:S(2)}) %collective-permute-start.15) | collective-permute-done | bytes 131104 | tf_op jit(solution)/shard_map/ppermute | solution.py:16
  250.4 0.6 copy-done.6
  251.0 0.6 copy-done.7
  251.7 17.1 %place_columns.1 = bf16[64,4096]{1,0:T(8,128)(2,1)} custom-call(bf16[2,64,512]{2,1,0:T(8,128)(2,1)} %fusion.8.refs_0_, bf16[2,64,512]{2,1,0:T(8,128)(2,1)} %copy-done.7, bf16[2,64,512]{2,1,0:T(8,128)(2,1)} %copy-done.6, bf16[2,64,512]{2,1,0:T(8,128)(2,1)} %copy-done.5), custom_call_target="tpu_custom_call" | custom-call | tf_op jit(solution)/shard_map/place_columns/pallas_call | solution.py:313
  (52 shorter events, 0.6 us)
Async XLA Ops:
  0.0 110.4 %copy-start = (s32[16]{0:T(128)S(1)}, s32[16]{0:T(128)}, u32[]{:S(2)}) copy-start(s32[16]{0:T(128)} %param.12) | copy-start | bytes 196
  1.4 104.7 %copy-start.1 = (bf16[128,16,128]{2,1,0:T(8,128)(2,1)S(1)}, bf16[128,16,128]{2,1,0:T(8,128)(2,1)}, u32[]{:S(2)}) copy-start(bf16[128,16,128]{2,1,0:T(8,128)(2,1)} %param.8) | copy-start | bytes 1572868
  1.4 107.6 %copy-start.4 = (s32[16,32]{1,0:T(8,128)S(1)}, s32[16,32]{1,0:T(8,128)}, u32[]{:S(2)}) copy-start(s32[16,32]{1,0:T(8,128)} %slot_ref.1) | copy-start | bytes 6148
  1.4 107.7 %copy-start.8 = (s32[8,1,2]{0,2,1:T(2,128)S(1)}, s32[8,1,2]{0,2,1:T(2,128)}, u32[]{:S(2)}) copy-start(s32[8,1,2]{0,2,1:T(2,128)} %param.14) | copy-start | bytes 196
  101.4 15.2 %collective-permute-start = (bf16[8,2,128,128]{3,2,1,0:T(8,128)(2,1)}, bf16[8,2,128,128]{3,2,1,0:T(8,128)(2,1)S(1)}, u32[]{:S(2)}, u32[]{:S(2)}) collective-permute-start(bf16[8,2,128,128]{3,2,1,0:T(8,128)(2,1)} %get-tuple-element.20), channel_id=1, source_target_pairs={{0,2},{2,0},{4,6},{6,4},{8,10},{10,8},{12,14},{14,12},{1,3},{3,1},... | collective-permute-start | bytes 1572872 | tf_op jit(solution)/shard_map/ppermute | solution.py:16
  104.4 26.3 %collective-permute-start.1 = (bf16[8,2,128,128]{3,2,1,0:T(8,128)(2,1)}, bf16[8,2,128,128]{3,2,1,0:T(8,128)(2,1)S(1)}, u32[]{:S(2)}, u32[]{:S(2)}) collective-permute-start(bf16[8,2,128,128]{3,2,1,0:T(8,128)(2,1)} %get-tuple-element.21), channel_id=1, source_target_pairs={{0,4},{2,6},{4,0},{6,2},{8,12},{10,14},{12,8},{14,10},{1,5},{3,7},... | collective-permute-start | bytes 1572872 | tf_op jit(solution)/shard_map/ppermute | solution.py:16
  106.0 34.3 %collective-permute-start.2 = (bf16[8,2,128,128]{3,2,1,0:T(8,128)(2,1)}, bf16[8,2,128,128]{3,2,1,0:T(8,128)(2,1)S(1)}, u32[]{:S(2)}, u32[]{:S(2)}) collective-permute-start(bf16[8,2,128,128]{3,2,1,0:T(8,128)(2,1)} %get-tuple-element.22), channel_id=1, source_target_pairs={{0,6},{2,4},{4,2},{6,0},{8,14},{10,12},{12,10},{14,8},{1,7},{3,5},... | collective-permute-start | bytes 1572872 | tf_op jit(solution)/shard_map/ppermute | solution.py:16
  106.0 37.8 %collective-permute-start.6 = (bf16[2048,128]{1,0:T(8,128)(2,1)S(1)}, bf16[2048,128]{1,0:T(8,128)(2,1)S(1)}, u32[]{:S(2)}, u32[]{:S(2)}) collective-permute-start(bf16[2048,128]{1,0:T(8,128)(2,1)S(1)} %bitcast.67), channel_id=1, source_target_pairs={{0,8},{2,10},{4,12},{6,14},{8,0},{10,2},{12,4},{14,6},{1,9},{3,11}... | collective-permute-start | bytes 1572872 | tf_op jit(solution)/shard_map/ppermute | solution.py:16
  140.3 31.2 %copy-start.2 = (bf16[128,1,128]{2,0,1:T(8,128)(2,1)S(1)}, bf16[128,1,128]{2,0,1:T(8,128)(2,1)}, u32[]{:S(2)}) copy-start(bf16[128,1,128]{2,0,1:T(8,128)(2,1)} %param.9) | copy-start | bytes 98308
  140.3 31.2 %copy-start.3 = (bf16[128,1,128]{2,0,1:T(8,128)(2,1)S(1)}, bf16[128,1,128]{2,0,1:T(8,128)(2,1)}, u32[]{:S(2)}) copy-start(bf16[128,1,128]{2,0,1:T(8,128)(2,1)} %param.10) | copy-start | bytes 98308
  140.3 22.7 %collective-permute-start.3 = (bf16[8,2,128,128]{3,2,1,0:T(8,128)(2,1)}, bf16[8,2,128,128]{3,2,1,0:T(8,128)(2,1)S(1)}, u32[]{:S(2)}, u32[]{:S(2)}) collective-permute-start(bf16[8,2,128,128]{3,2,1,0:T(8,128)(2,1)} %get-tuple-element.23), channel_id=1, source_target_pairs={{0,2},{2,0},{4,6},{6,4},{8,10},{10,8},{12,14},{14,12},{1,3},{3,1},... | collective-permute-start | bytes 1572872 | tf_op jit(solution)/shard_map/ppermute | solution.py:16
  142.0 21.0 %collective-permute-start.4 = (bf16[8,2,128,128]{3,2,1,0:T(8,128)(2,1)}, bf16[8,2,128,128]{3,2,1,0:T(8,128)(2,1)S(1)}, u32[]{:S(2)}, u32[]{:S(2)}) collective-permute-start(bf16[8,2,128,128]{3,2,1,0:T(8,128)(2,1)} %get-tuple-element.24), channel_id=1, source_target_pairs={{0,4},{2,6},{4,0},{6,2},{8,12},{10,14},{12,8},{14,10},{1,5},{3,7},... | collective-permute-start | bytes 1572872 | tf_op jit(solution)/shard_map/ppermute | solution.py:16
  142.0 29.6 %collective-permute-start.5 = (bf16[8,2,128,128]{3,2,1,0:T(8,128)(2,1)}, bf16[8,2,128,128]{3,2,1,0:T(8,128)(2,1)S(1)}, u32[]{:S(2)}, u32[]{:S(2)}) collective-permute-start(bf16[8,2,128,128]{3,2,1,0:T(8,128)(2,1)} %get-tuple-element.25), channel_id=1, source_target_pairs={{0,6},{2,4},{4,2},{6,0},{8,14},{10,12},{12,10},{14,8},{1,7},{3,5},... | collective-permute-start | bytes 1572872 | tf_op jit(solution)/shard_map/ppermute | solution.py:16
  155.9 33.1 %collective-permute-start.7 = (bf16[2096,128]{1,0:T(8,128)(2,1)S(1)}, bf16[2096,128]{1,0:T(8,128)(2,1)S(1)}, u32[]{:S(2)}, u32[]{:S(2)}) collective-permute-start(bf16[2096,128]{1,0:T(8,128)(2,1)S(1)} %attend_partner.1), channel_id=1, source_target_pairs={{0,8},{2,10},{4,12},{6,14},{8,0},{10,2},{12,4},{14,6},{1,9},{3,11}... | collective-permute-start | bytes 1609736 | tf_op jit(solution)/shard_map/ppermute | solution.py:16
  171.5 60.4 %collective-permute-start.8 = (bf16[2048,512]{1,0:T(8,128)(2,1)}, bf16[2048,512]{1,0:T(8,128)(2,1)S(1)}, u32[]{:S(2)}, u32[]{:S(2)}) collective-permute-start(bf16[2048,512]{1,0:T(8,128)(2,1)} %param.15), channel_id=1, source_target_pairs={{0,2},{2,0},{4,6},{6,4},{8,10},{10,8},{12,14},{14,12},{1,3},{3,1},... | collective-permute-start | bytes 6291464 | tf_op jit(solution)/shard_map/ppermute | solution.py:16
  189.6 20.9 %collective-permute-start.10 = (bf16[128,2048]{1,0:T(8,128)(2,1)S(1)}, bf16[128,2048]{1,0:T(8,128)(2,1)S(1)}, u32[]{:S(2)}, u32[]{:S(2)}) collective-permute-start(bf16[128,2048]{1,0:T(8,128)(2,1)S(1)} %combine.1), channel_id=1, source_target_pairs={{0,8},{2,10},{4,12},{6,14},{8,0},{10,2},{12,4},{14,6},{1,9},{3,11}... | collective-permute-start | bytes 1572872 | tf_op jit(solution)/shard_map/ppermute | solution.py:16
  189.7 27.3 %collective-permute-start.13 = (bf16[128,2048]{1,0:T(8,128)(2,1)S(1)}, bf16[128,2048]{1,0:T(8,128)(2,1)}, u32[]{:S(2)}, u32[]{:S(2)}) collective-permute-start(bf16[128,2048]{1,0:T(8,128)(2,1)S(1)} %combine.1), channel_id=1, source_target_pairs={{0,4},{2,6},{4,0},{6,2},{8,12},{10,14},{12,8},{14,10},{1,5},{3,7},... | collective-permute-start | bytes 1572872 | tf_op jit(solution)/shard_map/ppermute | solution.py:16
  210.5 17.3 %collective-permute-start.16 = (bf16[128,2048]{1,0:T(8,128)(2,1)S(1)}, bf16[128,2048]{1,0:T(8,128)(2,1)S(1)}, u32[]{:S(2)}, u32[]{:S(2)}) collective-permute-start(bf16[128,2048]{1,0:T(8,128)(2,1)S(1)} %collective-permute-done.10), channel_id=1, source_target_pairs={{0,4},{2,6},{4,0},{6,2},{8,12},{10,14},{12,8},{14,10},{1,5},{3,7},... | collective-permute-start | bytes 1572872 | tf_op jit(solution)/shard_map/ppermute | solution.py:16
  232.5 6.6 %collective-permute-start.17 = (bf16[2,64,512]{2,1,0:T(8,128)(2,1)S(1)}, bf16[2,64,512]{2,1,0:T(8,128)(2,1)S(1)}, u32[]{:S(2)}, u32[]{:S(2)}) collective-permute-start(bf16[2,64,512]{2,1,0:T(8,128)(2,1)S(1)} %pad_maximum_fusion.3), channel_id=1, source_target_pairs={{0,1},{1,0},{2,3},{3,2},{4,5},{5,4},{6,7},{7,6},{8,9},{9,8},{10,11... | collective-permute-start | bytes 393224 | tf_op jit(solution)/shard_map/ppermute | solution.py:16
  234.0 5.2 %collective-permute-start.14 = (bf16[2,64,512]{2,1,0:T(8,128)(2,1)S(1)}, bf16[2,64,512]{2,1,0:T(8,128)(2,1)S(1)}, u32[]{:S(2)}, u32[]{:S(2)}) collective-permute-start(bf16[2,64,512]{2,1,0:T(8,128)(2,1)S(1)} %pad_maximum_fusion.2), channel_id=1, source_target_pairs={{0,1},{1,0},{2,3},{3,2},{4,5},{5,4},{6,7},{7,6},{8,9},{9,8},{10,11... | collective-permute-start | bytes 393224 | tf_op jit(solution)/shard_map/ppermute | solution.py:16
  235.1 4.3 %collective-permute-start.11 = (bf16[2,64,512]{2,1,0:T(8,128)(2,1)S(1)}, bf16[2,64,512]{2,1,0:T(8,128)(2,1)S(1)}, u32[]{:S(2)}, u32[]{:S(2)}) collective-permute-start(bf16[2,64,512]{2,1,0:T(8,128)(2,1)S(1)} %pad_maximum_fusion.1), channel_id=1, source_target_pairs={{0,1},{1,0},{2,3},{3,2},{4,5},{5,4},{6,7},{7,6},{8,9},{9,8},{10,11... | collective-permute-start | bytes 393224 | tf_op jit(solution)/shard_map/ppermute | solution.py:16
  235.7 8.1 %collective-permute-start.9 = (bf16[2,64,512]{2,1,0:T(8,128)(2,1)S(1)}, bf16[2,64,512]{2,1,0:T(8,128)(2,1)S(1)}, u32[]{:S(2)}, u32[]{:S(2)}) collective-permute-start(bf16[2,64,512]{2,1,0:T(8,128)(2,1)S(1)} %pad_maximum_fusion), channel_id=1, source_target_pairs={{0,1},{1,0},{2,3},{3,2},{4,5},{5,4},{6,7},{7,6},{8,9},{9,8},{10,11... | collective-permute-start | bytes 393224 | tf_op jit(solution)/shard_map/ppermute | solution.py:16
  239.1 8.3 %collective-permute-start.18 = (bf16[2,64,512]{2,1,0:T(8,128)(2,1)S(1)}, bf16[2,64,512]{2,1,0:T(8,128)(2,1)S(1)}, u32[]{:S(2)}, u32[]{:S(2)}) collective-permute-start(bf16[2,64,512]{2,1,0:T(8,128)(2,1)S(1)} %fusion.11), channel_id=1, source_target_pairs={{0,12},{2,14},{4,8},{6,10},{8,4},{10,6},{12,0},{14,2},{1,13},{3,15... | collective-permute-start | bytes 393224 | tf_op jit(solution)/shard_map/ppermute | solution.py:16
  239.3 11.1 %collective-permute-start.15 = (bf16[2,64,512]{2,1,0:T(8,128)(2,1)S(1)}, bf16[2,64,512]{2,1,0:T(8,128)(2,1)S(1)}, u32[]{:S(2)}, u32[]{:S(2)}) collective-permute-start(bf16[2,64,512]{2,1,0:T(8,128)(2,1)S(1)} %fusion.10), channel_id=1, source_target_pairs={{0,4},{2,6},{4,0},{6,2},{8,12},{10,14},{12,8},{14,10},{1,5},{3,7},... | collective-permute-start | bytes 393224 | tf_op jit(solution)/shard_map/ppermute | solution.py:16
  239.4 11.0 %collective-permute-start.12 = (bf16[2,64,512]{2,1,0:T(8,128)(2,1)S(1)}, bf16[2,64,512]{2,1,0:T(8,128)(2,1)S(1)}, u32[]{:S(2)}, u32[]{:S(2)}) collective-permute-start(bf16[2,64,512]{2,1,0:T(8,128)(2,1)S(1)} %fusion.9), channel_id=1, source_target_pairs={{0,8},{2,10},{4,12},{6,14},{8,0},{10,2},{12,4},{14,6},{1,9},{3,11}... | collective-permute-start | bytes 393224 | tf_op jit(solution)/shard_map/ppermute | solution.py:16
  247.4 2.9 %copy-start.5 = (bf16[2,64,512]{2,1,0:T(8,128)(2,1)}, bf16[2,64,512]{2,1,0:T(8,128)(2,1)S(1)}, u32[]{:S(2)}) copy-start(bf16[2,64,512]{2,1,0:T(8,128)(2,1)S(1)} %collective-permute-done.18.refs_3_) | copy-start | bytes 393220
  250.4 0.7 copy-start.6
  251.0 0.6 copy-start.7

commit v2 on v1

v2 whole, which is shorter than its diff:
```python
import functools
import math

import jax
import jax.numpy as jnp
from jax import lax
from jax.experimental import pallas as pl
from jax.experimental.pallas import tpu as pltpu
from jax.sharding import PartitionSpec as P

LOW = -1e30
VMEM_LIMIT = 48 * 1024 * 1024


def swap(array, axis, size, mask):
    return lax.ppermute(array, axis, [(i, i ^ mask) for i in range(size)])


def pack_kernel(masks, partner, per_peer, slot_ref, ids_ref, kv_ref, *rest):
    outs, (table, sems) = rest[:-2], rest[-2:]
    me = lax.axis_index("req")
    clusters, pieces = slot_ref.shape
    held = kv_ref.shape[0]
    picks = ids_ref.shape[0]
    low = me * held

    def scan(c, carry):
        count = jnp.int32(0)
        for p in range(pieces):
            slot = slot_ref[c, p] - low
            table[c, count] = slot
            count = count + ((slot >= 0) & (slot < held)).astype(jnp.int32)
        return carry

    lax.fori_loop(0, clusters, scan, 0)
    copies = []
    for part in range(2):
        for index, mask in enumerate(masks):
            request = me ^ mask
            if part == 0:
                request = request ^ partner
            out = outs[part * len(masks) + index]
            for s in range(picks):
                c = ids_ref[s, request]
                for k in range(per_peer):
                    copies.append(
                        pltpu.make_async_copy(
                            kv_ref.at[table[c, k], 0], out.at[s * per_peer + k], sems.at[len(copies)]
                        )
                    )
                    copies[-1].start()
    for copy in copies:
        copy.wait()


def pack(piece_slot, plan, cluster_kv, masks, partner, per_peer):
    count = plan.shape[0] * per_peer
    shape = jax.ShapeDtypeStruct((count,) + cluster_kv.shape[2:], cluster_kv.dtype)
    smem = pl.BlockSpec(memory_space=pltpu.SMEM)
    total = 2 * len(masks)
    size = total * count * math.prod(cluster_kv.shape[2:]) * 2
    return pl.pallas_call(
        functools.partial(pack_kernel, masks, partner, per_peer),
        out_shape=[shape] * total,
        in_specs=[smem, smem, pl.BlockSpec(memory_space=pl.ANY)],
        out_specs=[pl.BlockSpec(memory_space=pltpu.VMEM)] * total,
        scratch_shapes=[
            pltpu.SMEM((piece_slot.shape[0], per_peer + 1), jnp.int32),
            pltpu.SemaphoreType.DMA((total * count,)),
        ],
        compiler_params=pltpu.CompilerParams(vmem_limit_bytes=VMEM_LIMIT),
        cost_estimate=pl.CostEstimate(flops=0, bytes_accessed=2 * size, transcendentals=0),
        name="pack_pieces",
    )(piece_slot, plan, cluster_kv)


def attend_kernel(settings, *refs):
    own, heads, block, rows_step, sources, scale, mode, earlier, packed = settings
    refs = list(refs)

    def take(n):
        taken, refs[:] = refs[:n], refs[n:]
        return taken

    q_ref, valid_ref = take(2)
    slot_ref, pool_ref = take(2) if 0 in sources else (None, None)
    own_k, own_v = take(2) if own else (None, None)
    got = dict(zip([j for j in sources if j], take(len([j for j in sources if j]))))
    before = take(2) if earlier else None
    other = take(1)[0] if packed else None
    outs = take(2 if mode == "state" else 1)
    kv, bias, scores, tops, total, mixed, lse, sem = refs
    rows, size = q_ref.shape
    keys = kv.shape[2]
    each = valid_ref.shape[1]
    lane = lax.broadcasted_iota(jnp.int32, (1, keys), 1)
    lines = rows // keys

    def piece(j, e):
        return got[j].at[e] if j else pool_ref.at[slot_ref[e], 0]

    at = jnp.int32(0)
    for j in sources:
        for e in range(each):
            valid = valid_ref[j, e]

            @pl.when(valid > 0)
            def _(j=j, e=e, valid=valid, at=at):
                pltpu.make_async_copy(piece(j, e), kv.at[at], sem).start()
                bias[at] = jnp.where(lane < valid, 0.0, LOW)

            at = at + (valid > 0).astype(jnp.int32)
    count = at
    blocks = (count + block - 1) // block
    for extra in range(block - 1):
        spot = count + extra

        @pl.when(spot < blocks * block)
        def _(spot=spot):
            pltpu.make_async_copy(piece(sources[0], 0), kv.at[spot], sem).start()
            bias[spot] = jnp.full((1, keys), LOW, jnp.float32)

    def wait(i, carry):
        pltpu.make_async_copy(piece(sources[0], 0), kv.at[0], sem).wait()
        return carry

    lax.fori_loop(0, blocks * block, wait, 0)

    def load(b, which):
        return kv[pl.ds(b * block, block), which].reshape(block * keys, size)

    def fold(values, op):
        parts = [values[:, i * keys : (i + 1) * keys] for i in range(values.shape[1] // keys)]
        while len(parts) > 1:
            parts = [op(parts[i], parts[i + 1]) if i + 1 < len(parts) else parts[i] for i in range(0, len(parts), 2)]
        return parts[0]

    def score(i, b):
        q = q_ref[pl.ds(i * rows_step, rows_step), :]
        s = lax.dot_general(q, load(b, 0), (((1,), (1,)), ((), ())), preferred_element_type=jnp.float32)
        line = bias[pl.ds(b * block, block)]
        s = s * scale + jnp.concatenate([line[n] for n in range(block)], axis=1)
        scores[i % 2, b] = s
        tops[i % 2] = jnp.maximum(tops[i % 2], fold(s, jnp.maximum))

    def start(i):
        if own:
            q = q_ref[pl.ds(i * rows_step, rows_step), :]
            s = lax.dot_general(q, own_k[...], (((1,), (1,)), ((), ())), preferred_element_type=jnp.float32)
            position = (lax.broadcasted_iota(jnp.int32, s.shape, 0) + i * rows_step) // heads
            s = jnp.where(position >= lax.broadcasted_iota(jnp.int32, s.shape, 1), s * scale, LOW)
            scores[i % 2, scores.shape[1] - 1, :, : s.shape[1]] = s
            tops[i % 2] = fold(s, jnp.maximum)
        else:
            tops[i % 2] = jnp.full(tops.shape[1:], LOW, jnp.float32)

    def weigh(i, b, top):
        p = jnp.exp2(scores[i % 2, b] - top)
        total[...] += fold(p, jnp.add)
        mixed[...] += jnp.dot(p.astype(jnp.bfloat16), load(b, 1), preferred_element_type=jnp.float32)

    steps = rows // rows_step
    group = rows_step // keys
    eye = lax.broadcasted_iota(jnp.int32, (keys, keys), 0) == lax.broadcasted_iota(jnp.int32, (keys, keys), 1)

    def finish(i, top):
        row_sum = jnp.sum(total[...], axis=1, keepdims=True)
        some = row_sum > 0.0
        safe = jnp.where(some, row_sum, 1.0)
        normal = mixed[...] / safe
        first = i * rows_step
        here = pl.ds(first, rows_step)
        column = jnp.where(some, top + jnp.log2(safe), LOW)
        mine = jnp.concatenate(
            [
                jnp.sum(jnp.where(eye, column[n * keys : (n + 1) * keys], 0.0), axis=0, keepdims=True)
                for n in range(group)
            ],
            axis=0,
        )
        spots = pl.ds(i * group, group)
        rest = []
        if earlier:
            rest.append((before[0][here, :], before[1][spots, :]))
        if packed:
            logs = other[pl.ds(rows, 3 * lines), :].astype(jnp.float32)
            logs = sum(logs[n * lines + i * group : n * lines + (i + 1) * group] for n in range(3))
            rest.append((other[here, :].astype(jnp.float32), logs))
        if rest:
            peak = functools.reduce(jnp.maximum, [logs for _, logs in rest], mine)
            powers = [jnp.exp2(logs - peak) for _, logs in rest]
            whole = sum(powers, jnp.exp2(mine - peak))
            mine = peak + jnp.log2(whole)
            result = normal
            for (values, _), power in zip(rest, powers):
                share = power / whole
                wide = jnp.concatenate(
                    [
                        jnp.sum(jnp.where(eye, share[n : n + 1], 0.0), axis=1, keepdims=True)
                        for n in range(group)
                    ],
                    axis=0,
                )
                result = result + wide * (values - normal)
            normal = result
        if mode == "state":
            outs[0][here, :] = normal
            outs[1][spots, :] = mine
        elif mode == "packed":
            outs[0][here, :] = normal.astype(jnp.bfloat16)
            lse[spots, :] = mine
        else:
            mixed[...] = normal
            tokens = rows_step // heads
            for h in range(heads):
                outs[0][pl.ds(i * tokens, tokens), h * size : (h + 1) * size] = mixed[
                    pl.ds(h, tokens, stride=heads), :
                ].astype(jnp.bfloat16)

    for i in range(steps + 1):
        top = None
        if i > 0:
            top = jnp.max(tops[(i - 1) % 2], axis=1, keepdims=True)
            if own:
                p = jnp.exp2(scores[(i - 1) % 2, scores.shape[1] - 1, :, : own_k.shape[0]] - top)
                total[...] = fold(p, jnp.add)
                mixed[...] = jnp.dot(p.astype(jnp.bfloat16), own_v[...], preferred_element_type=jnp.float32)
            else:
                total[...] = jnp.zeros(total.shape, jnp.float32)
                mixed[...] = jnp.zeros(mixed.shape, jnp.float32)
        if i < steps:
            start(i)

        def body(b, carry, i=i, top=top):
            if i < steps:
                score(i, b)
            if i > 0:
                weigh(i - 1, b, top)
            return carry

        lax.fori_loop(0, blocks, body, 0)
        if i > 0:
            finish(i - 1, top)
    if mode == "packed":
        left = lse[...]
        for n in range(3):
            part = left.astype(jnp.bfloat16)
            outs[0][pl.ds(rows + n * lines, lines), :] = part
            left = left - part.astype(jnp.float32)


def attend(name, mode, heads, q, valid, got, local=None, own=None, earlier=None, packed=None):
    rows, size = q.shape
    each = valid.shape[1]
    sources = ([0] if local is not None else []) + list(got)
    keys = size
    block = 4
    rows_step = math.gcd(rows, 512)
    lines = rows // keys
    scale = size ** -0.5 * math.log2(math.e)
    settings = (
        own is not None, heads, block, rows_step, sources, scale, mode, earlier is not None, packed is not None
    )
    smem = pl.BlockSpec(memory_space=pltpu.SMEM)
    vmem = pl.BlockSpec(memory_space=pltpu.VMEM)
    anywhere = pl.BlockSpec(memory_space=pl.ANY)
    operands, in_specs = [q, valid], [vmem, smem]
    if local is not None:
        operands, in_specs = operands + list(local), in_specs + [smem, anywhere]
    if own is not None:
        operands, in_specs = operands + list(own), in_specs + [vmem] * 2
    operands, in_specs = operands + list(got.values()), in_specs + [anywhere] * len(got)
    if earlier is not None:
        operands, in_specs = operands + list(earlier), in_specs + [vmem] * 2
    if packed is not None:
        operands, in_specs = operands + [packed], in_specs + [vmem]
    if mode == "state":
        out_shape = [
            jax.ShapeDtypeStruct((rows, size), jnp.float32),
            jax.ShapeDtypeStruct((lines, keys), jnp.float32),
        ]
    elif mode == "packed":
        out_shape = [jax.ShapeDtypeStruct((rows + 3 * lines, size), jnp.bfloat16)]
    else:
        out_shape = [jax.ShapeDtypeStruct((rows // heads, heads * size), jnp.bfloat16)]
    most = -(-len(sources) * each // block)
    shape = (2, keys, size)
    work = rows * len(sources) * each * keys
    out = pl.pallas_call(
        functools.partial(attend_kernel, settings),
        out_shape=out_shape,
        in_specs=in_specs,
        out_specs=[vmem] * len(out_shape),
        scratch_shapes=[
            pltpu.VMEM((most * block,) + shape, q.dtype),
            pltpu.VMEM((most * block, 1, keys), jnp.float32),
            pltpu.VMEM((2, most + (1 if own is not None else 0), rows_step, block * keys), jnp.float32),
            pltpu.VMEM((2, rows_step, keys), jnp.float32),
            pltpu.VMEM((rows_step, keys), jnp.float32),
            pltpu.VMEM((rows_step, size), jnp.float32),
            pltpu.VMEM((lines, keys), jnp.float32),
            pltpu.SemaphoreType.DMA,
        ],
        compiler_params=pltpu.CompilerParams(vmem_limit_bytes=VMEM_LIMIT),
        cost_estimate=pl.CostEstimate(flops=8 * work * size, bytes_accessed=4 << 20, transcendentals=work),
        name=name,
    )(*operands)
    return out if mode == "state" else out[0]


def project_kernel(attended, w_mine, w_pair, away, keep, scratch):
    core = lax.axis_index("head")
    share = away.shape[1]
    for side, w in enumerate((w_mine, w_pair)):
        scratch[side] = jnp.dot(attended[...], w[...], preferred_element_type=jnp.float32)
        away[side] = scratch[side, pl.ds(pl.multiple_of((core ^ 1) * share, share), share), :].astype(jnp.bfloat16)
        keep[side] = scratch[side, pl.ds(pl.multiple_of(core * share, share), share), :]


def project(attended, w_mine, w_pair, cores):
    tokens, depth = attended.shape
    width = w_mine.shape[1]
    share = tokens // cores
    vmem = pl.BlockSpec(memory_space=pltpu.VMEM)
    return pl.pallas_call(
        project_kernel,
        out_shape=[
            jax.ShapeDtypeStruct((2, share, width), jnp.bfloat16),
            jax.ShapeDtypeStruct((2, share, width), jnp.float32),
        ],
        in_specs=[vmem] * 3,
        out_specs=[vmem] * 2,
        scratch_shapes=[pltpu.VMEM((2, tokens, width), jnp.float32)],
        compiler_params=pltpu.CompilerParams(vmem_limit_bytes=VMEM_LIMIT),
        cost_estimate=pl.CostEstimate(
            flops=4 * tokens * depth * width, bytes_accessed=4 * depth * width, transcendentals=0
        ),
        name="project",
    )(attended, w_mine, w_pair)


def place_kernel(masks, *refs):
    parts, out = refs[:-1], refs[-1]
    me = lax.axis_index("req")
    width = parts[0].shape[2]
    for part, mask in zip(parts, masks):
        for side in range(2):
            column = ((me ^ mask) ^ side) * width
            out[:, pl.ds(pl.multiple_of(column, width), width)] = part[side]


def place(parts, masks):
    _, rows, width = parts[0].shape
    vmem = pl.BlockSpec(memory_space=pltpu.VMEM)
    return pl.pallas_call(
        functools.partial(place_kernel, masks),
        out_shape=jax.ShapeDtypeStruct((rows, 2 * len(parts) * width), parts[0].dtype),
        in_specs=[vmem] * len(parts),
        out_specs=vmem,
        compiler_params=pltpu.CompilerParams(vmem_limit_bytes=VMEM_LIMIT),
        name="place_columns",
    )(*parts)


def local(queries, new_keys, new_values, cluster_kv, cluster_len, piece_slot, cluster_ids, w_out):
    me = lax.axis_index("req")
    core = lax.axis_index("head")
    peers = lax.axis_size("req")
    cores = lax.axis_size("head")
    tokens, heads, size = queries.shape
    held = cluster_kv.shape[0]
    keys = cluster_kv.shape[3]
    pieces = piece_slot.shape[1]
    per_peer = pieces // peers
    half = peers // 2
    masks = list(range(1, half))

    plan = cluster_ids[:, 0]
    packed = pack(piece_slot, plan.T, cluster_kv, masks, half, per_peer)
    q_mine = queries.reshape(tokens * heads, size)
    q_theirs = swap(q_mine, "req", peers, half)
    got_theirs = [swap(a, "req", peers, m) for a, m in zip(packed[: len(masks)], masks)]

    owner = piece_slot // held
    position = jnp.arange(pieces, dtype=jnp.int32)
    same = (owner[:, :, None] == owner[:, None, :]) & (position[:, None] > position[None, :])[None]
    rank = jnp.sum(same.astype(jnp.int32), axis=2)

    def tables(request):
        chosen = lax.dynamic_index_in_dim(plan, request, 0, keepdims=False)
        own_owner, own_rank, own_slot = owner[chosen], rank[chosen], piece_slot[chosen] % held
        sender = me ^ jnp.arange(half, dtype=jnp.int32)
        fits = (own_owner[None, :, None, :] == sender[:, None, None, None]) & (
            own_rank[None, :, None, :] == jnp.arange(per_peer, dtype=jnp.int32)[None, None, :, None]
        )
        filled = jnp.clip(cluster_len[chosen][:, None] - position[None, :] * keys, 0, keys)
        valid = jnp.sum(jnp.where(fits, filled[None, :, None, :], 0), axis=3).reshape(half, -1)
        slots = jnp.sum(jnp.where(fits[0], own_slot[:, None, :], 0), axis=2).reshape(-1)
        return valid, slots

    valid_theirs, slots_theirs = tables(me ^ half)
    valid_mine, slots_mine = tables(me)

    got = dict(zip(masks, got_theirs))
    last, late = masks[-1:], masks[-2:-1]
    early = [m for m in masks if m not in last + late]

    def some(chosen):
        return {m: got[m] for m in chosen}

    state = attend(
        "attend_partner_early", "state", heads, q_theirs, valid_theirs, some(early), (slots_theirs, cluster_kv)
    )
    state = attend("attend_partner_late", "state", heads, q_theirs, valid_theirs, some(late), earlier=state)
    part = attend("attend_partner_last", "packed", heads, q_theirs, valid_theirs, some(last), earlier=state)

    later = lax.optimization_barrier((tuple(packed[len(masks) :]), tuple(got_theirs)))[0]
    got_mine = [swap(a, "req", peers, m) for a, m in zip(later, masks)]
    got = dict(zip(masks, got_mine))
    part = swap(part, "req", peers, half)
    w_later = lax.optimization_barrier((w_out, tuple(got_mine)))[0]
    w_pair = swap(w_later, "req", peers, 1)
    state = attend(
        "attend_own_local", "state", heads, q_mine, valid_mine, {}, (slots_mine, cluster_kv),
        (new_keys[:, 0], new_values[:, 0]),
    )
    if early:
        state = attend("attend_own_early", "state", heads, q_mine, valid_mine, some(early), earlier=state)
    state = attend("attend_own_late", "state", heads, q_mine, valid_mine, some(late), earlier=state)
    attended = attend(
        "attend_own_last", "final", heads, q_mine, valid_mine, some(last), earlier=state, packed=part
    )

    have = {0: attended}
    bit = half
    while bit > 1:
        for mask in list(have):
            have[mask ^ bit] = swap(have[mask], "req", peers, bit)
        bit //= 2

    results = {}
    for mask, rows in have.items():
        away, keep = project(rows, w_out, w_pair, cores)
        away = swap(away, "head", cores, 1)
        summed = (keep + away.astype(jnp.float32)).astype(jnp.bfloat16)
        results[mask] = swap(summed, "req", peers, mask) if mask else summed
    return place(list(results.values()), list(results))


def solution(mesh):
    return jax.shard_map(
        local,
        mesh=mesh,
        in_specs=(
            P(("groups", "req"), "head", None),
            P(("groups", "req"), "head", None),
            P(("groups", "req"), "head", None),
            P(("groups", "req"), "head", None, None, None),
            P("groups"),
            P("groups", None),
            P("groups", "head", None),
            P("head", "req"),
        ),
        out_specs=P(("groups", "req", "head"), None),
        check_vma=False,
    )
```

time: 271 us -> 193 us (0.71)
  Pallas kernels: 147 us -> 65.3 us
  waiting for transfers between devices: 56.1 us -> 93.1 us
  matrix products: 22.4 us -> 0 us
  starting transfers between devices: 32.6 us -> 22.5 us
    pallas_call x1, Pallas kernels: 100 us -> 6.35 us  [pack(): pl.pallas_call(functools.partial(pack_kernel, masks, partner, per_peer),...]
    ppermute x19, waiting for transfers between devices: 56.1 us -> 93.1 us  [swap(): return lax.ppermute(array, axis, [(i, i ^ mask) for i in range(size)])]
    pallas_call x2 -> x7, Pallas kernels: 29.5 us -> 55.1 us  [attend(): pl.pallas_call(functools.partial(attend_kernel, settings), out_shape=out_...]
    dot_general x16 -> x0, matrix products: 22.4 us -> none  [product(): jnp.dot(few, w, preferred_element_type=jnp.float32)]
    pallas_call x1, Pallas kernels: 17.1 us -> 0.84 us  [place(): pl.pallas_call(functools.partial(place_kernel, masks), out_shape=jax.Shap...]
    ppermute x19, starting transfers between devices: 32.6 us -> 22.5 us  [swap(): return lax.ppermute(array, axis, [(i, i ^ mask) for i in range(size)])]
  transfers between devices with their start and end apart: 19 -> 19, of which waited for: 9 -> 11; matrix products, arithmetic and copies ran while one was open for 11% -> 4% of each run, Pallas kernels for 11% -> 34%
where the time goes in v2:
time: 193 us; the launch traced here: 191 us
  waiting for transfers between devices  93.1 us (48%)
  Pallas kernels  65.3 us (34%)
  starting transfers between devices  22.5 us (12%)
  local copies, waits for them, and re-layouts  8.77 us (5%)
    ppermute x19, waiting for transfers between devices, swap(): return lax.ppermute(array, axis, [(i, i ^ mask) for i in range(size)])  93.1 us
    pallas_call x7, Pallas kernels, attend(): pl.pallas_call(functools.partial(attend_kernel, settings), out_shape=out_...  55.1 us
    ppermute x19, starting transfers between devices, swap(): return lax.ppermute(array, axis, [(i, i ^ mask) for i in range(size)])  22.5 us
    pallas_call x1, Pallas kernels, pack(): pl.pallas_call(functools.partial(pack_kernel, masks, partner, per_peer),...  6.35 us
  transfers between devices with their start and end apart: 19, of which 11 were waited for; matrix products, arithmetic and copies ran while one was open for 4% of the time, Pallas kernels for 34%

profile of v2, /device:TPU:0, one launch (start us, length us, event | category | flops | bytes accessed | tf_op | source)
XLA Modules:
  0.0 191.5 jit_solution(12773190910690743533)
XLA Ops:
  0.0 4.0 %collective-permute-start.6 = (bf16[2048,128]{1,0:T(8,128)(2,1)}, bf16[2048,128]{1,0:T(8,128)(2,1)S(1)}, u32[]{:S(2)}, u32[]{:S(2)}) collective-permute-start(bf16[2048,128]{1,0:T(8,128)(2,1)} %bitcast.23), channel_id=1, source_target_pairs={{0,8},{2,10},{4,12},{6,14},{8,0},{10,2},{12,4},{14,6},{1,9},{3,11}... | collective-permute-start | bytes 1572872 | tf_op jit(solution)/shard_map/ppermute | solution.py:16
  4.0 0.7 copy-done.3
  4.7 0.7 copy-done.5
  5.4 6.3 %pack_pieces.1 = (bf16[8,2,128,128]{3,2,1,0:T(8,128)(2,1)}, bf16[8,2,128,128]{3,2,1,0:T(8,128)(2,1)}, bf16[8,2,128,128]{3,2,1,0:T(8,128)(2,1)}, bf16[8,2,128,128...) custom-call(s32[16,32]{1,0:T(8,128)S(1)} %copy-done.3, ...), custom_call_target="tpu_custom_call" | custom-call | bytes 6291456 | tf_op jit(solution)/shard_map/pack_pieces/pallas_call | solution.py:62
  11.8 1.6 collective-permute-start
  13.4 1.6 collective-permute-start.1
  14.9 0.4 collective-permute-start.2
  15.3 0.2 dynamic-slice_reduce_fusion
  15.6 0.6 gather_fusion.3
  16.2 0.6 gather_fusion.2
  16.8 0.6 gather_fusion.6
  17.4 0.6 gather_fusion.7
  18.0 0.6 gather_fusion.4
  18.6 0.6 gather_fusion
  19.2 0.5 convert_reduce_fusion
  19.6 0.6 gather_fusion.5
  20.2 0.1 subtract_clamp_fusion
  20.3 0.1 broadcast_compare_fusion
  20.3 0.2 select_reduce_fusion
  20.6 0.6 gather_fusion.1
  21.2 0.2 select_reduce_fusion.1
  21.4 4.2 %collective-permute-done.refs_4_ = bf16[8,2,128,128]{3,2,1,0:T(8,128)(2,1)} collective-permute-done((bf16[8,2,128,128]{3,2,1,0:T(8,128)(2,1)}, bf16[8,2,128,128]{3,2,1,0:T(8,128)(2,1)}, u32[]{:S(2)}, u32[]{:S(2)}) %collective-permute-start) | collective-permute-done | bytes 524320 | tf_op jit(solution)/shard_map/ppermute | solution.py:16
  25.5 12.6 %collective-permute-done.1.refs_2_ = bf16[8,2,128,128]{3,2,1,0:T(8,128)(2,1)S(1)} collective-permute-done((bf16[8,2,128,128]{3,2,1,0:T(8,128)(2,1)}, bf16[8,2,128,128]{3,2,1,0:T(8,128)(2,1)S(1)}, u32[]{:S(2)}, u32[]{:S(2)}) %collective-permute-start.1) | collective-permute-done | bytes 524320 | tf_op jit(solution)/shard_map/ppermute | solution.py:16
  38.1 9.9 %collective-permute-done.2.refs_2_ = bf16[8,2,128,128]{3,2,1,0:T(8,128)(2,1)S(1)} collective-permute-done((bf16[8,2,128,128]{3,2,1,0:T(8,128)(2,1)}, bf16[8,2,128,128]{3,2,1,0:T(8,128)(2,1)S(1)}, u32[]{:S(2)}, u32[]{:S(2)}) %collective-permute-start.2) | collective-permute-done | bytes 524320 | tf_op jit(solution)/shard_map/ppermute | solution.py:16
  48.0 2.9 %collective-permute-start.4 = (bf16[8,2,128,128]{3,2,1,0:T(8,128)(2,1)S(1)}, bf16[8,2,128,128]{3,2,1,0:T(8,128)(2,1)}, u32[]{:S(2)}, u32[]{:S(2)}) collective-permute-start(bf16[8,2,128,128]{3,2,1,0:T(8,128)(2,1)S(1)} %get-tuple-element.40), channel_id=1, source_target_pairs={{0,4},{2,6},{4,0},{6,2},{8,12},{10,14},{12,8},{14,10},{1,5},{3,7},... | collective-permute-start | bytes 1572872 | tf_op jit(solution)/shard_map/ppermute | solution.py:16
  50.9 0.6 collective-permute-start.5
  51.5 0.1 select_reduce_fusion.2
  51.6 0.1 reshape.209.refs_1_
  51.7 0.1 reshape.210.refs_2_
  51.8 0.1 reshape.207.refs_1_
  51.9 0.2 select_reduce_fusion.3
  52.0 0.1 reshape.208.refs_2_
  52.1 9.2 %attend_partner_early.1 = (f32[2048,128]{1,0:T(8,128)S(1)}, f32[16,128]{1,0:T(8,128)S(1)}) custom-call(bf16[2048,128]{1,0:T(8,128)(2,1)S(1)} %collective-permute-done.6.refs_0_, s32[4,8]{1,0:T(4,128)S(1)} %reshape.209.refs_1_, s32[8]{0:T(128)S(1)} %reshape.210.refs_2_, bf16[64,1,2,128,128]{4,3,2,1,0:T(8,128)(2,1)} %refs_3_.3, ...), custom_call_target="tpu_custom_call" | custom-call | flops 4294967296 | bytes 4194304 | tf_op jit(solution)/shard_map/attend_partner_early/pallas_call | solution.py:289
  61.3 2.6 %collective-permute-done.3.refs_2_ = bf16[8,2,128,128]{3,2,1,0:T(8,128)(2,1)} collective-permute-done((bf16[8,2,128,128]{3,2,1,0:T(8,128)(2,1)S(1)}, bf16[8,2,128,128]{3,2,1,0:T(8,128)(2,1)}, u32[]{:S(2)}, u32[]{:S(2)}) %collective-permute-start.3) | collective-permute-done | bytes 524320 | tf_op jit(solution)/shard_map/ppermute | solution.py:16
  63.9 9.0 %collective-permute-done.4.refs_2_ = bf16[8,2,128,128]{3,2,1,0:T(8,128)(2,1)} collective-permute-done((bf16[8,2,128,128]{3,2,1,0:T(8,128)(2,1)S(1)}, bf16[8,2,128,128]{3,2,1,0:T(8,128)(2,1)}, u32[]{:S(2)}, u32[]{:S(2)}) %collective-permute-start.4) | collective-permute-done | bytes 524320 | tf_op jit(solution)/shard_map/ppermute | solution.py:16
  72.9 1.4 collective-permute-start.8
  74.3 7.8 %attend_partner_late.1 = (f32[2048,128]{1,0:T(8,128)S(1)}, f32[16,128]{1,0:T(8,128)S(1)}) custom-call(bf16[2048,128]{1,0:T(8,128)(2,1)S(1)} %collective-permute-done.6.refs_0_, s32[4,8]{1,0:T(4,128)S(1)} %reshape.209.refs_1_, bf16[8,2,128,128]{3,2,1,0:T(8,128)(2,1)S(1)} %collective-permute-done.1.refs_2_, f32[2048,128]{1,0:T(8,128)S(1)} %get-tuple-element.48.refs_3_, ...), custom_call_target="tpu_custom_call" | custom-call | flops 2147483648 | bytes 4194304 | tf_op jit(solution)/shard_map/attend_partner_late/pallas_call | solution.py:289
  82.1 5.3 %attend_partner_last.1 = bf16[2096,128]{1,0:T(8,128)(2,1)S(1)} custom-call(bf16[2048,128]{1,0:T(8,128)(2,1)S(1)} %collective-permute-done.6.refs_0_, s32[4,8]{1,0:T(4,128)S(1)} %reshape.209.refs_1_, bf16[8,2,128,128]{3,2,1,0:T(8,128)(2,1)S(1)} %collective-permute-done.2.refs_2_, f32[2048,128]{1,0:T(8,128)S(1)} %get-tuple-element.50.refs_3_, ...), custom_call_target="tpu_custom_call" | custom-call | flops 2147483648 | bytes 4194304 | tf_op jit(solution)/shard_map/attend_partner_last/pallas_call | solution.py:289
  87.5 2.5 %collective-permute-start.7 = (bf16[2096,128]{1,0:T(8,128)(2,1)S(1)}, bf16[2096,128]{1,0:T(8,128)(2,1)S(1)}, u32[]{:S(2)}, u32[]{:S(2)}) collective-permute-start(bf16[2096,128]{1,0:T(8,128)(2,1)S(1)} %attend_partner_last.1), channel_id=1, source_target_pairs={{0,8},{2,10},{4,12},{6,14},{8,0},{10,2},{12,4},{14,6},{1,9},{3,11}... | collective-permute-start | bytes 1609736 | tf_op jit(solution)/shard_map/ppermute | solution.py:16
  90.0 2.2 %copy-done.2 = bf16[64,1,2,128,128]{4,3,2,1,0:T(8,128)(2,1)S(1)} copy-done((bf16[64,1,2,128,128]{4,3,2,1,0:T(8,128)(2,1)S(1)}, bf16[64,1,2,128,128]{4,3,2,1,0:T(8,128)(2,1)}, u32[]{:S(2)}) %copy-start.2) | copy-done | bytes 4194328
  92.2 7.4 %attend_own_local.1 = (f32[2048,128]{1,0:T(8,128)S(1)}, f32[16,128]{1,0:T(8,128)S(1)}) custom-call(bf16[2048,128]{1,0:T(8,128)(2,1)S(1)} %bitcast.24, s32[4,8]{1,0:T(4,128)S(1)} %reshape.207.refs_1_, s32[8]{0:T(128)S(1)} %reshape.208.refs_2_, bf16[64,1,2,128,128]{4,3,2,1,0:T(8,128)(2,1)S(1)} %copy-done.2, bf16[128,128]{1,0:T(8,128)(2,1)S(1)} %bitcast.28, ...), custom_call_target="tpu_custom_call" | custom-call | flops 2147483648 | bytes 4194304 | tf_op jit(solution)/shard_map/attend_own_local/pallas_call | solution.py:289
  99.6 8.1 %attend_own_early.1 = (f32[2048,128]{1,0:T(8,128)S(1)}, f32[16,128]{1,0:T(8,128)S(1)}) custom-call(bf16[2048,128]{1,0:T(8,128)(2,1)S(1)} %bitcast.25, s32[4,8]{1,0:T(4,128)S(1)} %reshape.207.refs_1_, bf16[8,2,128,128]{3,2,1,0:T(8,128)(2,1)} %collective-permute-done.5.refs_2_, f32[2048,128]{1,0:T(8,128)S(1)} %get-tuple-element.42.refs_3_, ...), custom_call_target="tpu_custom_call" | custom-call | flops 2147483648 | bytes 4194304 | tf_op jit(solution)/shard_map/attend_own_early/pallas_call | solution.py:289
  107.7 8.0 %attend_own_late.1 = (f32[2048,128]{1,0:T(8,128)S(1)}, f32[16,128]{1,0:T(8,128)S(1)}) custom-call(bf16[2048,128]{1,0:T(8,128)(2,1)S(1)} %bitcast.26, s32[4,8]{1,0:T(4,128)S(1)} %reshape.207.refs_1_, bf16[8,2,128,128]{3,2,1,0:T(8,128)(2,1)} %collective-permute-done.4.refs_2_, f32[2048,128]{1,0:T(8,128)S(1)} %get-tuple-element.44.refs_3_, ...), custom_call_target="tpu_custom_call" | custom-call | flops 2147483648 | bytes 4194304 | tf_op jit(solution)/shard_map/attend_own_late/pallas_call | solution.py:289
  115.8 9.2 %attend_own_last.1.attended = bf16[128,2048]{1,0:T(8,128)(2,1)S(1)} custom-call(bf16[2048,128]{1,0:T(8,128)(2,1)S(1)} %bitcast.27, s32[4,8]{1,0:T(4,128)S(1)} %reshape.207.refs_1_, bf16[8,2,128,128]{3,2,1,0:T(8,128)(2,1)} %collective-permute-done.3.refs_2_, f32[2048,128]{1,0:T(8,128)S(1)} %get-tuple-element.46.refs_3_, ...), custom_call_target="tpu_custom_call" | custom-call | flops 2147483648 | bytes 4194304 | tf_op jit(solution)/shard_map/attend_own_last/pallas_call | solution.py:289
  124.9 0.1 collective-permute-start.10
  125.0 23.4 %collective-permute-done.10.attended = bf16[128,2048]{1,0:T(8,128)(2,1)S(1)} collective-permute-done((bf16[128,2048]{1,0:T(8,128)(2,1)S(1)}, bf16[128,2048]{1,0:T(8,128)(2,1)S(1)}, u32[]{:S(2)}, u32[]{:S(2)}) %collective-permute-start.10) | collective-permute-done | bytes 524320 | tf_op jit(solution)/shard_map/ppermute | solution.py:16
  148.4 2.0 %collective-permute-start.13 = (bf16[128,2048]{1,0:T(8,128)(2,1)S(1)}, bf16[128,2048]{1,0:T(8,128)(2,1)S(1)}, u32[]{:S(2)}, u32[]{:S(2)}) collective-permute-start(bf16[128,2048]{1,0:T(8,128)(2,1)S(1)} %attend_own_last.1.attended), channel_id=1, source_target_pairs={{0,4},{2,6},{4,0},{6,2},{8,12},{10,14},{12,8},{14,10},{1,5},{3,7},... | collective-permute-start | bytes 1572872 | tf_op jit(solution)/shard_map/ppermute | solution.py:16
  150.4 12.8 %collective-permute-done.16.attended = bf16[128,2048]{1,0:T(8,128)(2,1)S(1)} collective-permute-done((bf16[128,2048]{1,0:T(8,128)(2,1)S(1)}, bf16[128,2048]{1,0:T(8,128)(2,1)S(1)}, u32[]{:S(2)}, u32[]{:S(2)}) %collective-permute-start.16) | collective-permute-done | bytes 524320 | tf_op jit(solution)/shard_map/ppermute | solution.py:16
  163.2 0.8 project.7
  163.9 0.1 collective-permute-start.17
  164.0 9.4 %collective-permute-done.13.attended = bf16[128,2048]{1,0:T(8,128)(2,1)S(1)} collective-permute-done((bf16[128,2048]{1,0:T(8,128)(2,1)S(1)}, bf16[128,2048]{1,0:T(8,128)(2,1)S(1)}, u32[]{:S(2)}, u32[]{:S(2)}) %collective-permute-start.13) | collective-permute-done | bytes 524320 | tf_op jit(solution)/shard_map/ppermute | solution.py:16
  173.5 0.8 project.6
  174.2 0.1 collective-permute-start.14
  174.3 0.8 project.5
  175.1 0.6 collective-permute-start.11
  175.7 0.8 project.4
  176.4 0.1 collective-permute-start.9
  176.6 2.3 %collective-permute-start.18 = (bf16[2,64,512]{2,1,0:T(8,128)(2,1)S(1)}, bf16[2,64,512]{2,1,0:T(8,128)(2,1)S(1)}, u32[]{:S(2)}, u32[]{:S(2)}) collective-permute-start(bf16[2,64,512]{2,1,0:T(8,128)(2,1)S(1)} %add_convert_fusion), channel_id=1, source_target_pairs={{0,12},{2,14},{4,8},{6,10},{8,4},{10,6},{12,0},{14,2},{1,13},{3,15... | collective-permute-start | bytes 393224 | tf_op jit(solution)/shard_map/ppermute | solution.py:16
  178.9 0.1 collective-permute-start.15
  179.0 2.2 %collective-permute-start.12 = (bf16[2,64,512]{2,1,0:T(8,128)(2,1)S(1)}, bf16[2,64,512]{2,1,0:T(8,128)(2,1)S(1)}, u32[]{:S(2)}, u32[]{:S(2)}) collective-permute-start(bf16[2,64,512]{2,1,0:T(8,128)(2,1)S(1)} %add_convert_fusion.2), channel_id=1, source_target_pairs={{0,8},{2,10},{4,12},{6,14},{8,0},{10,2},{12,4},{14,6},{1,9},{3,11}... | collective-permute-start | bytes 393224 | tf_op jit(solution)/shard_map/ppermute | solution.py:16
  181.2 3.5 %collective-permute-done.18.refs_3_ = bf16[2,64,512]{2,1,0:T(8,128)(2,1)S(1)} collective-permute-done((bf16[2,64,512]{2,1,0:T(8,128)(2,1)S(1)}, bf16[2,64,512]{2,1,0:T(8,128)(2,1)S(1)}, u32[]{:S(2)}, u32[]{:S(2)}) %collective-permute-start.18) | collective-permute-done | bytes 131104 | tf_op jit(solution)/shard_map/ppermute | solution.py:16
  184.8 4.7 %collective-permute-done.15.refs_2_ = bf16[2,64,512]{2,1,0:T(8,128)(2,1)S(1)} collective-permute-done((bf16[2,64,512]{2,1,0:T(8,128)(2,1)S(1)}, bf16[2,64,512]{2,1,0:T(8,128)(2,1)S(1)}, u32[]{:S(2)}, u32[]{:S(2)}) %collective-permute-start.15) | collective-permute-done | bytes 131104 | tf_op jit(solution)/shard_map/ppermute | solution.py:16
  189.4 1.2 collective-permute-done.12.refs_1_
  190.6 0.8 place_columns.1
  (42 shorter events, 0.3 us)
Async XLA Ops:
  0.0 16.2 %copy-start = (s32[16]{0:T(128)S(1)}, s32[16]{0:T(128)}, u32[]{:S(2)}) copy-start(s32[16]{0:T(128)} %param.12) | copy-start | bytes 196
  0.0 52.1 %collective-permute-start.6 = (bf16[2048,128]{1,0:T(8,128)(2,1)}, bf16[2048,128]{1,0:T(8,128)(2,1)S(1)}, u32[]{:S(2)}, u32[]{:S(2)}) collective-permute-start(bf16[2048,128]{1,0:T(8,128)(2,1)} %bitcast.23), channel_id=1, source_target_pairs={{0,8},{2,10},{4,12},{6,14},{8,0},{10,2},{12,4},{14,6},{1,9},{3,11}... | collective-permute-start | bytes 1572872 | tf_op jit(solution)/shard_map/ppermute | solution.py:16
  4.0 0.7 copy-start.3
  4.7 0.7 copy-start.5
  5.4 9.9 %copy-start.6 = (s32[8,1,2]{0,2,1:T(2,128)S(1)}, s32[8,1,2]{0,2,1:T(2,128)}, u32[]{:S(2)}) copy-start(s32[8,1,2]{0,2,1:T(2,128)} %param.14) | copy-start | bytes 196
  5.4 10.2 %copy-start.4 = (s32[16,32]{1,0:T(8,128)S(1)}, s32[16,32]{1,0:T(8,128)}, u32[]{:S(2)}) copy-start(s32[16,32]{1,0:T(8,128)} %slot_ref.1) | copy-start | bytes 6148
  11.8 13.8 %collective-permute-start = (bf16[8,2,128,128]{3,2,1,0:T(8,128)(2,1)}, bf16[8,2,128,128]{3,2,1,0:T(8,128)(2,1)}, u32[]{:S(2)}, u32[]{:S(2)}) collective-permute-start(bf16[8,2,128,128]{3,2,1,0:T(8,128)(2,1)} %get-tuple-element.36), channel_id=1, source_target_pairs={{0,2},{2,0},{4,6},{6,4},{8,10},{10,8},{12,14},{14,12},{1,3},{3,1},... | collective-permute-start | bytes 1572872 | tf_op jit(solution)/shard_map/ppermute | solution.py:16
  13.4 24.7 %collective-permute-start.1 = (bf16[8,2,128,128]{3,2,1,0:T(8,128)(2,1)}, bf16[8,2,128,128]{3,2,1,0:T(8,128)(2,1)S(1)}, u32[]{:S(2)}, u32[]{:S(2)}) collective-permute-start(bf16[8,2,128,128]{3,2,1,0:T(8,128)(2,1)} %get-tuple-element.37), channel_id=1, source_target_pairs={{0,4},{2,6},{4,0},{6,2},{8,12},{10,14},{12,8},{14,10},{1,5},{3,7},... | collective-permute-start | bytes 1572872 | tf_op jit(solution)/shard_map/ppermute | solution.py:16
  14.9 33.0 %collective-permute-start.2 = (bf16[8,2,128,128]{3,2,1,0:T(8,128)(2,1)}, bf16[8,2,128,128]{3,2,1,0:T(8,128)(2,1)S(1)}, u32[]{:S(2)}, u32[]{:S(2)}) collective-permute-start(bf16[8,2,128,128]{3,2,1,0:T(8,128)(2,1)} %get-tuple-element.38), channel_id=1, source_target_pairs={{0,6},{2,4},{4,2},{6,0},{8,14},{10,12},{12,10},{14,8},{1,7},{3,5},... | collective-permute-start | bytes 1572872 | tf_op jit(solution)/shard_map/ppermute | solution.py:16
  48.0 15.9 %collective-permute-start.3 = (bf16[8,2,128,128]{3,2,1,0:T(8,128)(2,1)S(1)}, bf16[8,2,128,128]{3,2,1,0:T(8,128)(2,1)}, u32[]{:S(2)}, u32[]{:S(2)}) collective-permute-start(bf16[8,2,128,128]{3,2,1,0:T(8,128)(2,1)S(1)} %get-tuple-element.39), channel_id=1, source_target_pairs={{0,6},{2,4},{4,2},{6,0},{8,14},{10,12},{12,10},{14,8},{1,7},{3,5},... | collective-permute-start | bytes 1572872 | tf_op jit(solution)/shard_map/ppermute | solution.py:16
  48.0 24.9 %collective-permute-start.4 = (bf16[8,2,128,128]{3,2,1,0:T(8,128)(2,1)S(1)}, bf16[8,2,128,128]{3,2,1,0:T(8,128)(2,1)}, u32[]{:S(2)}, u32[]{:S(2)}) collective-permute-start(bf16[8,2,128,128]{3,2,1,0:T(8,128)(2,1)S(1)} %get-tuple-element.40), channel_id=1, source_target_pairs={{0,4},{2,6},{4,0},{6,2},{8,12},{10,14},{12,8},{14,10},{1,5},{3,7},... | collective-permute-start | bytes 1572872 | tf_op jit(solution)/shard_map/ppermute | solution.py:16
  50.9 21.9 %collective-permute-start.5 = (bf16[8,2,128,128]{3,2,1,0:T(8,128)(2,1)S(1)}, bf16[8,2,128,128]{3,2,1,0:T(8,128)(2,1)}, u32[]{:S(2)}, u32[]{:S(2)}) collective-permute-start(bf16[8,2,128,128]{3,2,1,0:T(8,128)(2,1)S(1)} %get-tuple-element.41), channel_id=1, source_target_pairs={{0,2},{2,0},{4,6},{6,4},{8,10},{10,8},{12,14},{14,12},{1,3},{3,1},... | collective-permute-start | bytes 1572872 | tf_op jit(solution)/shard_map/ppermute | solution.py:16
  52.1 20.8 %copy-start.1 = (bf16[2048,512]{1,0:T(8,128)(2,1)S(1)}, bf16[2048,512]{1,0:T(8,128)(2,1)}, u32[]{:S(2)}) copy-start(bf16[2048,512]{1,0:T(8,128)(2,1)} %w_mine.7) | copy-start | bytes 6291460
  72.9 90.3 %collective-permute-start.8 = (bf16[2048,512]{1,0:T(8,128)(2,1)S(1)}, bf16[2048,512]{1,0:T(8,128)(2,1)S(1)}, u32[]{:S(2)}, u32[]{:S(2)}) collective-permute-start(bf16[2048,512]{1,0:T(8,128)(2,1)S(1)} %copy-done.1), channel_id=1, source_target_pairs={{0,2},{2,0},{4,6},{6,4},{8,10},{10,8},{12,14},{14,12},{1,3},{3,1},... | collective-permute-start | bytes 6291464 | tf_op jit(solution)/shard_map/ppermute | solution.py:16
  82.1 7.9 %copy-start.7 = (bf16[128,16,128]{2,1,0:T(8,128)(2,1)S(1)}, bf16[128,16,128]{2,1,0:T(8,128)(2,1)}, u32[]{:S(2)}) copy-start(bf16[128,16,128]{2,1,0:T(8,128)(2,1)} %param.8) | copy-start | bytes 1572868
  82.1 7.9 %copy-start.8 = (bf16[128,1,128]{2,0,1:T(8,128)(2,1)S(1)}, bf16[128,1,128]{2,0,1:T(8,128)(2,1)}, u32[]{:S(2)}) copy-start(bf16[128,1,128]{2,0,1:T(8,128)(2,1)} %param.9) | copy-start | bytes 98308
  82.1 7.9 %copy-start.9 = (bf16[128,1,128]{2,0,1:T(8,128)(2,1)S(1)}, bf16[128,1,128]{2,0,1:T(8,128)(2,1)}, u32[]{:S(2)}) copy-start(bf16[128,1,128]{2,0,1:T(8,128)(2,1)} %param.10) | copy-start | bytes 98308
  87.5 28.3 %collective-permute-start.7 = (bf16[2096,128]{1,0:T(8,128)(2,1)S(1)}, bf16[2096,128]{1,0:T(8,128)(2,1)S(1)}, u32[]{:S(2)}, u32[]{:S(2)}) collective-permute-start(bf16[2096,128]{1,0:T(8,128)(2,1)S(1)} %attend_partner_last.1), channel_id=1, source_target_pairs={{0,8},{2,10},{4,12},{6,14},{8,0},{10,2},{12,4},{14,6},{1,9},{3,11}... | collective-permute-start | bytes 1609736 | tf_op jit(solution)/shard_map/ppermute | solution.py:16
  90.0 2.2 %copy-start.2 = (bf16[64,1,2,128,128]{4,3,2,1,0:T(8,128)(2,1)S(1)}, bf16[64,1,2,128,128]{4,3,2,1,0:T(8,128)(2,1)}, u32[]{:S(2)}) copy-start(bf16[64,1,2,128,128]{4,3,2,1,0:T(8,128)(2,1)} %refs_3_.3) | copy-start | bytes 12582916
  124.9 23.4 %collective-permute-start.10 = (bf16[128,2048]{1,0:T(8,128)(2,1)S(1)}, bf16[128,2048]{1,0:T(8,128)(2,1)S(1)}, u32[]{:S(2)}, u32[]{:S(2)}) collective-permute-start(bf16[128,2048]{1,0:T(8,128)(2,1)S(1)} %attend_own_last.1.attended), channel_id=1, source_target_pairs={{0,8},{2,10},{4,12},{6,14},{8,0},{10,2},{12,4},{14,6},{1,9},{3,11}... | collective-permute-start | bytes 1572872 | tf_op jit(solution)/shard_map/ppermute | solution.py:16
  148.4 14.8 %collective-permute-start.16 = (bf16[128,2048]{1,0:T(8,128)(2,1)S(1)}, bf16[128,2048]{1,0:T(8,128)(2,1)S(1)}, u32[]{:S(2)}, u32[]{:S(2)}) collective-permute-start(bf16[128,2048]{1,0:T(8,128)(2,1)S(1)} %collective-permute-done.10.attended), channel_id=1, source_target_pairs={{0,4},{2,6},{4,0},{6,2},{8,12},{10,14},{12,8},{14,10},{1,5},{3,7},... | collective-permute-start | bytes 1572872 | tf_op jit(solution)/shard_map/ppermute | solution.py:16
  148.4 25.1 %collective-permute-start.13 = (bf16[128,2048]{1,0:T(8,128)(2,1)S(1)}, bf16[128,2048]{1,0:T(8,128)(2,1)S(1)}, u32[]{:S(2)}, u32[]{:S(2)}) collective-permute-start(bf16[128,2048]{1,0:T(8,128)(2,1)S(1)} %attend_own_last.1.attended), channel_id=1, source_target_pairs={{0,4},{2,6},{4,0},{6,2},{8,12},{10,14},{12,8},{14,10},{1,5},{3,7},... | collective-permute-start | bytes 1572872 | tf_op jit(solution)/shard_map/ppermute | solution.py:16
  163.9 12.6 %collective-permute-start.17 = (bf16[2,64,512]{2,1,0:T(8,128)(2,1)S(1)}, bf16[2,64,512]{2,1,0:T(8,128)(2,1)S(1)}, u32[]{:S(2)}, u32[]{:S(2)}) collective-permute-start(bf16[2,64,512]{2,1,0:T(8,128)(2,1)S(1)} %get-tuple-element.60), channel_id=1, source_target_pairs={{0,1},{1,0},{2,3},{3,2},{4,5},{5,4},{6,7},{7,6},{8,9},{9,8},{10,11... | collective-permute-start | bytes 393224 | tf_op jit(solution)/shard_map/ppermute | solution.py:16
  174.2 4.6 %collective-permute-start.14 = (bf16[2,64,512]{2,1,0:T(8,128)(2,1)S(1)}, bf16[2,64,512]{2,1,0:T(8,128)(2,1)S(1)}, u32[]{:S(2)}, u32[]{:S(2)}) collective-permute-start(bf16[2,64,512]{2,1,0:T(8,128)(2,1)S(1)} %get-tuple-element.58), channel_id=1, source_target_pairs={{0,1},{1,0},{2,3},{3,2},{4,5},{5,4},{6,7},{7,6},{8,9},{9,8},{10,11... | collective-permute-start | bytes 393224 | tf_op jit(solution)/shard_map/ppermute | solution.py:16
  175.1 3.9 %collective-permute-start.11 = (bf16[2,64,512]{2,1,0:T(8,128)(2,1)S(1)}, bf16[2,64,512]{2,1,0:T(8,128)(2,1)S(1)}, u32[]{:S(2)}, u32[]{:S(2)}) collective-permute-start(bf16[2,64,512]{2,1,0:T(8,128)(2,1)S(1)} %get-tuple-element.56), channel_id=1, source_target_pairs={{0,1},{1,0},{2,3},{3,2},{4,5},{5,4},{6,7},{7,6},{8,9},{9,8},{10,11... | collective-permute-start | bytes 393224 | tf_op jit(solution)/shard_map/ppermute | solution.py:16
  176.4 4.8 %collective-permute-start.9 = (bf16[2,64,512]{2,1,0:T(8,128)(2,1)S(1)}, bf16[2,64,512]{2,1,0:T(8,128)(2,1)S(1)}, u32[]{:S(2)}, u32[]{:S(2)}) collective-permute-start(bf16[2,64,512]{2,1,0:T(8,128)(2,1)S(1)} %get-tuple-element.54), channel_id=1, source_target_pairs={{0,1},{1,0},{2,3},{3,2},{4,5},{5,4},{6,7},{7,6},{8,9},{9,8},{10,11... | collective-permute-start | bytes 393224 | tf_op jit(solution)/shard_map/ppermute | solution.py:16
  176.6 8.2 %collective-permute-start.18 = (bf16[2,64,512]{2,1,0:T(8,128)(2,1)S(1)}, bf16[2,64,512]{2,1,0:T(8,128)(2,1)S(1)}, u32[]{:S(2)}, u32[]{:S(2)}) collective-permute-start(bf16[2,64,512]{2,1,0:T(8,128)(2,1)S(1)} %add_convert_fusion), channel_id=1, source_target_pairs={{0,12},{2,14},{4,8},{6,10},{8,4},{10,6},{12,0},{14,2},{1,13},{3,15... | collective-permute-start | bytes 393224 | tf_op jit(solution)/shard_map/ppermute | solution.py:16
  178.9 10.6 %collective-permute-start.15 = (bf16[2,64,512]{2,1,0:T(8,128)(2,1)S(1)}, bf16[2,64,512]{2,1,0:T(8,128)(2,1)S(1)}, u32[]{:S(2)}, u32[]{:S(2)}) collective-permute-start(bf16[2,64,512]{2,1,0:T(8,128)(2,1)S(1)} %add_convert_fusion.1), channel_id=1, source_target_pairs={{0,4},{2,6},{4,0},{6,2},{8,12},{10,14},{12,8},{14,10},{1,5},{3,7},... | collective-permute-start | bytes 393224 | tf_op jit(solution)/shard_map/ppermute | solution.py:16
  179.0 11.6 %collective-permute-start.12 = (bf16[2,64,512]{2,1,0:T(8,128)(2,1)S(1)}, bf16[2,64,512]{2,1,0:T(8,128)(2,1)S(1)}, u32[]{:S(2)}, u32[]{:S(2)}) collective-permute-start(bf16[2,64,512]{2,1,0:T(8,128)(2,1)S(1)} %add_convert_fusion.2), channel_id=1, source_target_pairs={{0,8},{2,10},{4,12},{6,14},{8,0},{10,2},{12,4},{14,6},{1,9},{3,11}... | collective-permute-start | bytes 393224 | tf_op jit(solution)/shard_map/ppermute | solution.py:16
